TPU v7x, 256 devices: a whole 4x4x8 slice. The times are simulated.
256 devices in a mesh: lon: 32 (over y, x, core), lat: 8 (over z).
Axes of the slice: x: 4, y: 4, z: 8, core: 2. Of those that a mesh axis runs over, the one named last changes fastest.
Arguments:
- potential_warmth: float32 [12, 128, 4096], P(None, 'lat', 'lon'), may hold values from -6 to 6
- salt_anomaly_value: float32 [12, 128, 4096], P(None, 'lat', 'lon'), may hold values from -6 to 6
- zonal_current_speed: float32 [12, 128, 4096], P(None, 'lat', 'lon'), may hold values from -1.8 to 1.8
- meridional_current_speed: float32 [12, 128, 4096], P(None, 'lat', 'lon'), may hold values from -1.8 to 1.8
- block_water_flag: int32 [8, 32], P('lat', 'lon'), may hold values 0 or 1
- water_point_flag: int32 [128, 4096], P('lat', 'lon'), may hold values 0 or 1
- wet_layer_count: int32 [128, 4096], P('lat', 'lon'), may hold values from 4 to 12
Outputs:
- temp_next: float32 [12, 128, 4096], P(None, 'lat', 'lon')
- salt_next: float32 [12, 128, 4096], P(None, 'lat', 'lon')
Inputs may be any that keep to these rules, and one draw needn't show every extreme that they name: `block_water_flag`: one entry a tile.
All inputs are finite; a program needn't handle non-finite values. No bound on the sum of `block_water_flag` or of `water_point_flag` on one device may be relied on, other than what follows from the above.
Results may differ from a plain program's by a relative error of at most 0.0003.
Values sent between devices are 32-bit elements; how exact they have to be, the bound alone decides.
A program may use at most 64 MiB of HBM per device.

v0:
```python
import jax
import jax.numpy as jnp
from jax import lax
from jax.sharding import PartitionSpec as P

time_step = 0.5
diffusivity = 0.1
strat_floor = 0.5
slope_limit = 2.0
thermal_coef = 0.2
haline_coef = 0.8


def with_halo(block, sides, width, periodic):
    for axis, dim in sides:
        count = lax.axis_size(axis)
        forward = [(i, i + 1) for i in range(count - 1)]
        if periodic:
            forward.append((count - 1, 0))
        backward = [(target, source) for source, target in forward]
        low = lax.ppermute(
            lax.slice_in_dim(block, block.shape[dim] - width, None, axis=dim), axis, forward
        )
        high = lax.ppermute(lax.slice_in_dim(block, 0, width, axis=dim), axis, backward)
        block = jnp.concatenate([low, block, high], axis=dim)
    return block


def partner(array, axis, apart):
    return lax.ppermute(array, axis, [(i, i ^ 1 << apart) for i in range(lax.axis_size(axis))])


def trim_rim(grid_field, depth_cut):
    return grid_field[
        :, depth_cut : grid_field.shape[1] - depth_cut, depth_cut : grid_field.shape[2] - depth_cut
    ]


def positive_part(values):
    return jnp.maximum(values, 0.0)


def flux_div(flux_east, flux_north):
    return (
        flux_east[:, 1:-1, 1:]
        - flux_east[:, 1:-1, :-1]
        + (flux_north[:, 1:, 1:-1] - flux_north[:, :-1, 1:-1])
    )


def vert_div(flux_top):
    below = jnp.concatenate([flux_top[1:], jnp.zeros_like(flux_top[:1])], 0)
    return flux_top - below


def geometry(statics, layer_pile):
    u_cell = statics[:layer_pile]
    v_cell = statics[layer_pile : 2 * layer_pile]
    floor_level = statics[2 * layer_pile]
    level_index = jnp.arange(layer_pile).astype(statics.dtype)[:, None, None]
    wet_mask = (level_index < floor_level[None]).astype(statics.dtype)
    u_face = 0.5 * (u_cell[:, :, :-1] + u_cell[:, :, 1:]) * wet_mask[:, :, :-1] * wet_mask[:, :, 1:]
    v_face = 0.5 * (v_cell[:, :-1, :] + v_cell[:, 1:, :]) * wet_mask[:, :-1, :] * wet_mask[:, 1:, :]
    divergence = flux_div(u_face, v_face)
    w_top = -jnp.cumsum(divergence[::-1], 0)[::-1]
    return (trim_rim(wet_mask, 1), u_face[:, 1:-1, :], v_face[:, :, 1:-1], w_top)


def extreme_near(values, wet_mask, chooser):
    center = trim_rim(values, 1)
    center_wet = trim_rim(wet_mask, 1)
    result = center
    near_list = (
        (values[:, 1:-1, 2:], wet_mask[:, 1:-1, 2:]),
        (values[:, 1:-1, :-2], wet_mask[:, 1:-1, :-2]),
        (values[:, 2:, 1:-1], wet_mask[:, 2:, 1:-1]),
        (values[:, :-2, 1:-1], wet_mask[:, :-2, 1:-1]),
    )
    for near_vals, near_wet in near_list:
        result = chooser(result, jnp.where(near_wet > 0, near_vals, center))
    zero_row = jnp.zeros_like(center_wet[:1])
    above_vals = jnp.concatenate([center[:1], center[:-1]], 0)
    above_wet = jnp.concatenate([zero_row, center_wet[:-1]], 0)
    below_vals = jnp.concatenate([center[1:], center[-1:]], 0)
    below_wet = jnp.concatenate([center_wet[1:], zero_row], 0)
    result = chooser(result, jnp.where(above_wet > 0, above_vals, center))
    result = chooser(result, jnp.where(below_wet > 0, below_vals, center))
    return result


def limit_ratio(supply, headroom):
    return jnp.where(supply > headroom, headroom / jnp.where(supply > headroom, supply, 1.0), 1.0)


def advect(tracer, wet_mask, u_face, v_face, w_top):
    east_vel = u_face[:, :, 1:-1]
    north_vel = v_face[:, 1:-1, :]
    west_val = tracer[:, :, :-1]
    east_val = tracer[:, :, 1:]
    low_east = positive_part(east_vel) * west_val + jnp.minimum(east_vel, 0.0) * east_val
    anti_east = east_vel * 0.5 * (west_val + east_val) - low_east
    south_val = tracer[:, :-1, :]
    north_val = tracer[:, 1:, :]
    low_north = positive_part(north_vel) * south_val + jnp.minimum(north_vel, 0.0) * north_val
    anti_north = north_vel * 0.5 * (south_val + north_val) - low_north
    rise_vel = w_top[1:]
    upper_val = tracer[:-1]
    lower_val = tracer[1:]
    low_rise = positive_part(rise_vel) * lower_val + jnp.minimum(rise_vel, 0.0) * upper_val
    anti_rise = rise_vel * 0.5 * (upper_val + lower_val) - low_rise
    low_top = jnp.concatenate([w_top[:1] * tracer[:1], low_rise], 0)
    wet_one = trim_rim(wet_mask, 1)
    inner_val = trim_rim(tracer, 1)
    low_order = (
        inner_val - time_step * (flux_div(low_east, low_north) + trim_rim(vert_div(low_top), 1))
    ) * wet_one
    upper_bound = extreme_near(jnp.maximum(inner_val, low_order), wet_one, jnp.maximum)
    lower_bound = extreme_near(jnp.minimum(inner_val, low_order), wet_one, jnp.minimum)
    face_east = anti_east[:, 1:-1, 1:]
    face_west = anti_east[:, 1:-1, :-1]
    face_north = anti_north[:, 1:, 1:-1]
    face_south = anti_north[:, :-1, 1:-1]
    face_top = trim_rim(jnp.concatenate([jnp.zeros_like(anti_rise[:1]), anti_rise], 0), 1)
    face_bottom = jnp.concatenate([face_top[1:], jnp.zeros_like(face_top[:1])], 0)
    gain_in = (
        positive_part(face_west)
        + positive_part(-face_east)
        + positive_part(face_south)
        + positive_part(-face_north)
        + positive_part(face_bottom)
        + positive_part(-face_top)
    )
    gain_out = (
        positive_part(face_east)
        + positive_part(-face_west)
        + positive_part(face_north)
        + positive_part(-face_south)
        + positive_part(face_top)
        + positive_part(-face_bottom)
    )
    low_two = trim_rim(low_order, 1)
    ratio_in = limit_ratio(trim_rim(gain_in, 1), (upper_bound - low_two) / time_step)
    ratio_out = limit_ratio(trim_rim(gain_out, 1), (low_two - lower_bound) / time_step)
    anti_x2 = anti_east[:, 2:-2, 2:-2]
    limit_east = jnp.where(
        anti_x2 >= 0,
        jnp.minimum(ratio_in[:, :, 1:], ratio_out[:, :, :-1]),
        jnp.minimum(ratio_in[:, :, :-1], ratio_out[:, :, 1:]),
    )
    anti_y2 = anti_north[:, 2:-2, 2:-2]
    limit_north = jnp.where(
        anti_y2 >= 0,
        jnp.minimum(ratio_in[:, 1:, :], ratio_out[:, :-1, :]),
        jnp.minimum(ratio_in[:, :-1, :], ratio_out[:, 1:, :]),
    )
    anti_z2 = trim_rim(anti_rise, 2)
    limit_rise = jnp.where(
        anti_z2 >= 0,
        jnp.minimum(ratio_in[:-1], ratio_out[1:]),
        jnp.minimum(ratio_in[1:], ratio_out[:-1]),
    )
    limited_top = jnp.concatenate([jnp.zeros_like(anti_z2[:1]), limit_rise * anti_z2], 0)
    update = flux_div(limit_east * anti_x2, limit_north * anti_y2) + trim_rim(
        vert_div(limited_top), 1
    )
    return (trim_rim(low_order, 2) - time_step * update) * trim_rim(wet_mask, 3)


def vert_grad(grid_field, pair_wet, zero_row):
    return jnp.concatenate([zero_row, (grid_field[:-1] - grid_field[1:]) * pair_wet, zero_row], 0)


def pick_east(full_faces):
    top_faces = full_faces[:-1]
    bottom_faces = full_faces[1:]
    return [
        top_faces[:, :, :-1],
        bottom_faces[:, :, :-1],
        top_faces[:, :, 1:],
        bottom_faces[:, :, 1:],
    ]


def pick_north(full_faces):
    top_faces = full_faces[:-1]
    bottom_faces = full_faces[1:]
    return [
        top_faces[:, :-1, :],
        bottom_faces[:, :-1, :],
        top_faces[:, 1:, :],
        bottom_faces[:, 1:, :],
    ]


def stack_faces(part_vals, on_top):
    zero_row = jnp.zeros_like(part_vals[:1])
    if on_top:
        return jnp.concatenate([part_vals, zero_row], 0)
    return jnp.concatenate([zero_row, part_vals], 0)


def diffuse(scalar_quantities, wet_mask):
    temp_field, salt_field = scalar_quantities
    density = haline_coef * salt_field - thermal_coef * temp_field
    pair_east = wet_mask[:, :, :-1] * wet_mask[:, :, 1:]
    pair_north = wet_mask[:, :-1, :] * wet_mask[:, 1:, :]
    pair_rise = wet_mask[:-1] * wet_mask[1:]
    zero_row = jnp.zeros_like(wet_mask[:1])
    face_wet = jnp.concatenate([zero_row, pair_rise, zero_row], 0)
    rho_rise = vert_grad(density, pair_rise, zero_row)
    rho_east = (density[:, :, 1:] - density[:, :, :-1]) * pair_east
    rho_north = (density[:, 1:, :] - density[:, :-1, :]) * pair_north
    triads_east = []
    for rise_part, wet_part in zip(pick_east(rho_rise), pick_east(face_wet)):
        present = pair_east * wet_part
        slope_val = (
            jnp.clip(rho_east / jnp.maximum(-rise_part, strat_floor), -slope_limit, slope_limit)
            * present
        )
        triads_east.append((present, slope_val))
    triads_north = []
    for rise_part, wet_part in zip(pick_north(rho_rise), pick_north(face_wet)):
        present = pair_north * wet_part
        slope_val = (
            jnp.clip(rho_north / jnp.maximum(-rise_part, strat_floor), -slope_limit, slope_limit)
            * present
        )
        triads_north.append((present, slope_val))
    scale_flux = -diffusivity * 0.25
    results = []
    for tracer in scalar_quantities:
        grad_rise = vert_grad(tracer, pair_rise, zero_row)
        grad_east = (tracer[:, :, 1:] - tracer[:, :, :-1]) * pair_east
        grad_north = (tracer[:, 1:, :] - tracer[:, :-1, :]) * pair_north
        flux_east = jnp.zeros_like(grad_east)
        flux_north = jnp.zeros_like(grad_north)
        rise_total = jnp.zeros_like(trim_rim(face_wet, 1))
        for slot_index, ((present, slope_val), rise_part) in enumerate(
            zip(triads_east, pick_east(grad_rise))
        ):
            flux_east = flux_east + present * (grad_east + slope_val * rise_part)
            rise_vals = present * (slope_val * grad_east + slope_val * slope_val * rise_part)
            cell_vals = rise_vals[:, 1:-1, 1:] if slot_index < 2 else rise_vals[:, 1:-1, :-1]
            rise_total = rise_total + stack_faces(cell_vals, slot_index % 2 == 0)
        for slot_index, ((present, slope_val), rise_part) in enumerate(
            zip(triads_north, pick_north(grad_rise))
        ):
            flux_north = flux_north + present * (grad_north + slope_val * rise_part)
            rise_vals = present * (slope_val * grad_north + slope_val * slope_val * rise_part)
            cell_vals = rise_vals[:, 1:, 1:-1] if slot_index < 2 else rise_vals[:, :-1, 1:-1]
            rise_total = rise_total + stack_faces(cell_vals, slot_index % 2 == 0)
        rise_flux = scale_flux * rise_total
        update = flux_div(scale_flux * flux_east, scale_flux * flux_north) + (
            rise_flux[:-1] - rise_flux[1:]
        )
        results.append((trim_rim(tracer, 1) - time_step * update) * trim_rim(wet_mask, 1))
    return results


def extend_rim(grid_field, width, sign_flip):
    wide_field = with_halo(grid_field, (("lon", 2),), width, True)
    tall_field = with_halo(wide_field, (("lat", 1),), width, False)
    mirror_rows = wide_field[:, wide_field.shape[1] - width :, :]
    for bit_index in range(lax.axis_size("lon").bit_length() - 1):
        mirror_rows = partner(mirror_rows, "lon", bit_index)
    folded = mirror_rows[:, ::-1, ::-1] * sign_flip
    on_fold = lax.axis_index("lat") == lax.axis_size("lat") - 1
    north_rows = jnp.where(on_fold, folded, tall_field[:, tall_field.shape[1] - width :, :])
    return jnp.concatenate([tall_field[:, : tall_field.shape[1] - width, :], north_rows], 1)


def on_device(
    potential_warmth,
    salt_anomaly_value,
    zonal_current_speed,
    meridional_current_speed,
    block_water_flag,
    water_point_flag,
    wet_layer_count,
):
    layer_pile = potential_warmth.shape[0]
    floor_level = (wet_layer_count * water_point_flag * block_water_flag[0, 0]).astype(jnp.float32)
    statics = jnp.concatenate([zonal_current_speed, meridional_current_speed, floor_level[None]], 0)
    sign_flip = jnp.concatenate(
        [-jnp.ones((2 * layer_pile, 1, 1), jnp.float32), jnp.ones((1, 1, 1), jnp.float32)], 0
    )
    scalar_quantities = jnp.concatenate([potential_warmth, salt_anomaly_value], 0)
    wet_mask, u_face, v_face, w_top = geometry(extend_rim(statics, 4, sign_flip), layer_pile)
    wide_tracers = extend_rim(scalar_quantities, 3, 1.0)
    inner_moved = jnp.concatenate(
        [
            advect(wide_tracers[:layer_pile], wet_mask, u_face, v_face, w_top),
            advect(wide_tracers[layer_pile:], wet_mask, u_face, v_face, w_top),
        ],
        0,
    )
    refilled = extend_rim(inner_moved, 1, 1.0)
    advected = [refilled[:layer_pile], refilled[layer_pile:]]
    wet_one = trim_rim(wet_mask, 2)
    new_temp, new_salt = diffuse(advected, wet_one)
    return (new_temp, new_salt)


def solution(mesh):
    in_specs = (
        P(None, "lat", "lon"),
        P(None, "lat", "lon"),
        P(None, "lat", "lon"),
        P(None, "lat", "lon"),
        P("lat", "lon"),
        P("lat", "lon"),
        P("lat", "lon"),
    )
    out_specs = (P(None, "lat", "lon"), P(None, "lat", "lon"))
    return jax.shard_map(
        on_device, mesh=mesh, in_specs=in_specs, out_specs=out_specs, check_vma=False
    )
```

profile of v0, /device:TPU:96, one launch (start us, length us, event | category | flops | bytes accessed | tf_op | source)
XLA Modules:
  0.0 117.0 jit_solution(548006786206130642)
XLA Ops:
  0.6 0.9 constant_dynamic-update-slice_fusion.1
  1.9 5.1 %collective-permute-start.1 = (f32[24,16,3]{2,1,0:T(8,128)S(1)}, f32[24,16,3]{2,1,0:T(8,128)S(1)}, u32[]{:S(2)}, u32[]{:S(2)}) collective-permute-start(f32[24,16,3]{2,1,0:T(8,128)S(1)} %get-tuple-element.156), channel_id=1, source_target_pairs={{8,0},{16,8},{24,16},{32,24},{40,32},{48,40},{56,48},{64,56},{72,6... | collective-permute-start | bytes 13832 | tf_op jit(solution)/shard_map/ppermute | solution.py:24
  7.6 2.6 %collective-permute-done = f32[24,16,3]{2,1,0:T(8,128)S(1)} collective-permute-done((f32[24,16,3]{2,1,0:T(8,128)S(1)}, f32[24,16,3]{2,1,0:T(8,128)S(1)}, u32[]{:S(2)}, u32[]{:S(2)}) %collective-permute-start) | collective-permute-done | bytes 4640 | tf_op jit(solution)/shard_map/ppermute | solution.py:21
  10.7 5.1 %collective-permute-start.10 = (f32[25,16,4]{2,1,0:T(8,128)S(1)}, f32[25,16,4]{2,1,0:T(8,128)S(1)}, u32[]{:S(2)}, u32[]{:S(2)}) collective-permute-start(f32[25,16,4]{2,1,0:T(8,128)S(1)} %get-tuple-element.152), channel_id=1, source_target_pairs={{8,0},{16,8},{24,16},{32,24},{40,32},{48,40},{56,48},{64,56},{72,6... | collective-permute-start | bytes 19208 | tf_op jit(solution)/shard_map/ppermute | solution.py:24
  15.9 3.3 %collective-permute-done.10 = f32[25,16,4]{2,1,0:T(8,128)S(1)} collective-permute-done((f32[25,16,4]{2,1,0:T(8,128)S(1)}, f32[25,16,4]{2,1,0:T(8,128)S(1)}, u32[]{:S(2)}, u32[]{:S(2)}) %collective-permute-start.10) | collective-permute-done | bytes 6432 | tf_op jit(solution)/shard_map/ppermute | solution.py:24
  19.1 5.2 %collective-permute-done.9 = f32[25,16,4]{2,1,0:T(8,128)S(1)} collective-permute-done((f32[25,16,4]{2,1,0:T(8,128)S(1)}, f32[25,16,4]{2,1,0:T(8,128)S(1)}, u32[]{:S(2)}, u32[]{:S(2)}) %collective-permute-start.9) | collective-permute-done | bytes 6432 | tf_op jit(solution)/shard_map/ppermute | solution.py:21
  24.8 1.2 %collective-permute-done.12 = f32[25,4,136]{2,1,0:T(4,128)S(1)} collective-permute-done((f32[25,4,136]{2,1,0:T(4,128)S(1)}, f32[25,4,136]{2,1,0:T(4,128)S(1)}, u32[]{:S(2)}, u32[]{:S(2)}) %collective-permute-start.12) | collective-permute-done | bytes 54432 | tf_op jit(solution)/shard_map/ppermute | solution.py:30
  26.0 5.9 %collective-permute-done.5 = f32[24,3,134]{2,1,0:T(4,128)S(1)} collective-permute-done((f32[24,3,134]{2,1,0:T(4,128)S(1)}, f32[24,3,134]{2,1,0:T(4,128)S(1)}, u32[]{:S(2)}, u32[]{:S(2)}) %collective-permute-start.5) | collective-permute-done | bytes 38624 | tf_op jit(solution)/shard_map/ppermute | solution.py:30
  31.9 2.0 %collective-permute-start.8 = (f32[24,3,134]{2,1,0:T(4,128)S(1)}, f32[24,3,134]{2,1,0:T(4,128)S(1)}, u32[]{:S(2)}, u32[]{:S(2)}) collective-permute-start(f32[24,3,134]{2,1,0:T(4,128)S(1)} %get-tuple-element.97), channel_id=1, source_target_pairs={{1,0},{2,1},{3,2},{4,3},{5,4},{6,5},{7,6},{9,8},{10,9},{11,10},{12... | collective-permute-start | bytes 115784 | tf_op jit(solution)/shard_map/ppermute | solution.py:24
  34.1 3.2 %collective-permute-done.6 = f32[24,3,134]{2,1,0:T(4,128)S(1)} collective-permute-done((f32[24,3,134]{2,1,0:T(4,128)S(1)}, f32[24,3,134]{2,1,0:T(4,128)S(1)}, u32[]{:S(2)}, u32[]{:S(2)}) %collective-permute-start.6) | collective-permute-done | bytes 38624 | tf_op jit(solution)/shard_map/ppermute | solution.py:30
  37.3 5.0 %collective-permute-start.2 = (f32[24,3,134]{2,1,0:T(4,128)S(1)}, f32[24,3,134]{2,1,0:T(4,128)S(1)}, u32[]{:S(2)}, u32[]{:S(2)}) collective-permute-start(f32[24,3,134]{2,1,0:T(4,128)S(1)} %get-tuple-element.98), channel_id=1, source_target_pairs={{0,1},{1,2},{2,3},{3,4},{4,5},{5,6},{6,7},{8,9},{9,10},{10,11},{11... | collective-permute-start | bytes 115784 | tf_op jit(solution)/shard_map/ppermute | solution.py:21
  42.3 2.2 %collective-permute-start.11 = (f32[25,4,136]{2,1,0:T(4,128)S(1)}, f32[25,4,136]{2,1,0:T(4,128)S(1)}, u32[]{:S(2)}, u32[]{:S(2)}) collective-permute-start(f32[25,4,136]{2,1,0:T(4,128)S(1)} %get-tuple-element.81), channel_id=1, source_target_pairs={{0,1},{1,2},{2,3},{3,4},{4,5},{5,6},{6,7},{8,9},{9,10},{10,11},{11... | collective-permute-start | bytes 163208 | tf_op jit(solution)/shard_map/ppermute | solution.py:21
  44.5 3.7 %collective-permute-start.17 = (f32[25,4,136]{2,1,0:T(4,128)S(1)}, f32[25,4,136]{2,1,0:T(4,128)S(1)}, u32[]{:S(2)}, u32[]{:S(2)}) collective-permute-start(f32[25,4,136]{2,1,0:T(4,128)S(1)} %get-tuple-element.82), channel_id=1, source_target_pairs={{1,0},{2,1},{3,2},{4,3},{5,4},{6,5},{7,6},{9,8},{10,9},{11,10},{12... | collective-permute-start | bytes 163208 | tf_op jit(solution)/shard_map/ppermute | solution.py:24
  48.3 0.4 reverse
  48.8 4.5 %collective-permute-done.15 = f32[25,4,136]{2,1,0:T(4,128)S(1)} collective-permute-done((f32[25,4,136]{2,1,0:T(4,128)S(1)}, f32[25,4,136]{2,1,0:T(4,128)S(1)}, u32[]{:S(2)}, u32[]{:S(2)}) %collective-permute-start.15) | collective-permute-done | bytes 54432 | tf_op jit(solution)/shard_map/ppermute | solution.py:30
  53.3 3.2 %collective-permute-start.16 = (f32[25,4,136]{2,1,0:T(4,128)S(1)}, f32[25,4,136]{2,1,0:T(4,128)S(1)}, u32[]{:S(2)}, u32[]{:S(2)}) collective-permute-start(f32[25,4,136]{2,1,0:T(4,128)S(1)} %collective-permute-done.15), channel_id=1, source_target_pairs={{0,128},{8,136},{16,144},{24,152},{32,160},{40,168},{48,176},{56,1... | collective-permute-start | bytes 163208 | tf_op jit(solution)/shard_map/ppermute | solution.py:30
  56.8 0.3 copy-done.6
  57.1 2.3 %collective-permute-done.16 = f32[25,4,136]{2,1,0:T(4,128)S(1)} collective-permute-done((f32[25,4,136]{2,1,0:T(4,128)S(1)}, f32[25,4,136]{2,1,0:T(4,128)S(1)}, u32[]{:S(2)}, u32[]{:S(2)}) %collective-permute-start.16) | collective-permute-done | bytes 54432 | tf_op jit(solution)/shard_map/ppermute | solution.py:30
  59.4 0.4 reverse.1
  61.1 1.0 fusion.72
  62.7 1.7 %rev.17 = f32[12,22,134]{2,1,0:T(8,128)} reverse(f32[12,22,134]{2,1,0:T(8,128)} %fusion.72), dimensions={0} | reverse | bytes 283008 | tf_op jit(solution)/shard_map/rev | solution.py:65
  64.3 1.0 fusion.156
  65.5 0.8 copy-done.1
  66.5 1.1 slice_maximum_fusion.9
  70.6 1.3 %divide_select_fusion.1 = (f32[12,18,130]{2,1,0:T(8,128)S(1)}, pred[12,18,130]{2,1,0:T(8,128)(4,1)S(1)}, pred[12,18,130]{2,1,0:T(8,128)(4,1)S(1)}, pred[12,18,13...) fusion(f32[12,20,132]{2,1,0:T(8,128)S(1)} %get-tuple-element.10, ...), kind=kLoop, calls=%fused_computation.171 | loop fusion | flops 1095120 | bytes 2512320 | tf_op jit(solution)/shard_map/jit(_where)/select_n | solution.py:92
  71.9 1.0 divide_select_fusion.3
  72.9 1.0 divide_select_fusion.2
  73.8 1.0 divide_select_fusion
  74.8 0.6 fusion.38
  75.7 0.3 fusion.80
  76.0 0.4 fusion.128
  76.9 5.1 %collective-permute-start.19 = (f32[24,16,1]{2,1,0:T(8,128)S(1)}, f32[24,16,1]{2,1,0:T(8,128)S(1)}, u32[]{:S(2)}, u32[]{:S(2)}) collective-permute-start(f32[24,16,1]{2,1,0:T(8,128)S(1)} %get-tuple-element.154), channel_id=1, source_target_pairs={{8,0},{16,8},{24,16},{32,24},{40,32},{48,40},{56,48},{64,56},{72,6... | collective-permute-start | bytes 4616 | tf_op jit(solution)/shard_map/ppermute | solution.py:24
  81.9 3.3 %collective-permute-done.18 = f32[24,16,1]{2,1,0:T(8,128)S(1)} collective-permute-done((f32[24,16,1]{2,1,0:T(8,128)S(1)}, f32[24,16,1]{2,1,0:T(8,128)S(1)}, u32[]{:S(2)}, u32[]{:S(2)}) %collective-permute-start.18) | collective-permute-done | bytes 1568 | tf_op jit(solution)/shard_map/ppermute | solution.py:21
  85.6 1.2 %collective-permute-done.21 = f32[24,1,130]{2,1,0:T(1,128)S(1)} collective-permute-done((f32[24,1,130]{2,1,0:T(1,128)S(1)}, f32[24,1,130]{2,1,0:T(1,128)S(1)}, u32[]{:S(2)}, u32[]{:S(2)}) %collective-permute-start.21) | collective-permute-done | bytes 12512 | tf_op jit(solution)/shard_map/ppermute | solution.py:30
  86.8 3.8 %collective-permute-done.22 = f32[24,1,130]{2,1,0:T(1,128)S(1)} collective-permute-done((f32[24,1,130]{2,1,0:T(1,128)S(1)}, f32[24,1,130]{2,1,0:T(1,128)S(1)}, u32[]{:S(2)}, u32[]{:S(2)}) %collective-permute-start.22) | collective-permute-done | bytes 12512 | tf_op jit(solution)/shard_map/ppermute | solution.py:30
  90.6 0.3 collective-permute-start.23
  91.0 5.0 %collective-permute-done.23 = f32[24,1,130]{2,1,0:T(1,128)S(1)} collective-permute-done((f32[24,1,130]{2,1,0:T(1,128)S(1)}, f32[24,1,130]{2,1,0:T(1,128)S(1)}, u32[]{:S(2)}, u32[]{:S(2)}) %collective-permute-start.23) | collective-permute-done | bytes 12512 | tf_op jit(solution)/shard_map/ppermute | solution.py:30
  96.2 3.5 %collective-permute-done.24 = f32[24,1,130]{2,1,0:T(1,128)S(1)} collective-permute-done((f32[24,1,130]{2,1,0:T(1,128)S(1)}, f32[24,1,130]{2,1,0:T(1,128)S(1)}, u32[]{:S(2)}, u32[]{:S(2)}) %collective-permute-start.24) | collective-permute-done | bytes 12512 | tf_op jit(solution)/shard_map/ppermute | solution.py:30
  99.8 2.0 %collective-permute-start.25 = (f32[24,1,130]{2,1,0:T(1,128)S(1)}, f32[24,1,130]{2,1,0:T(1,128)S(1)}, u32[]{:S(2)}, u32[]{:S(2)}) collective-permute-start(f32[24,1,130]{2,1,0:T(1,128)S(1)} %collective-permute-done.24), channel_id=1, source_target_pairs={{0,128},{8,136},{16,144},{24,152},{32,160},{40,168},{48,176},{56,1... | collective-permute-start | bytes 37448 | tf_op jit(solution)/shard_map/ppermute | solution.py:30
  101.8 1.9 %collective-permute-start.26 = (f32[24,1,130]{2,1,0:T(1,128)S(1)}, f32[24,1,130]{2,1,0:T(1,128)S(1)}, u32[]{:S(2)}, u32[]{:S(2)}) collective-permute-start(f32[24,1,130]{2,1,0:T(1,128)S(1)} %get-tuple-element.93), channel_id=1, source_target_pairs={{1,0},{2,1},{3,2},{4,3},{5,4},{6,5},{7,6},{9,8},{10,9},{11,10},{12... | collective-permute-start | bytes 37448 | tf_op jit(solution)/shard_map/ppermute | solution.py:24
  103.7 5.1 %collective-permute-start.20 = (f32[24,1,130]{2,1,0:T(1,128)S(1)}, f32[24,1,130]{2,1,0:T(1,128)S(1)}, u32[]{:S(2)}, u32[]{:S(2)}) collective-permute-start(f32[24,1,130]{2,1,0:T(1,128)S(1)} %get-tuple-element.94), channel_id=1, source_target_pairs={{0,1},{1,2},{2,3},{3,4},{4,5},{5,6},{6,7},{8,9},{9,10},{10,11},{11... | collective-permute-start | bytes 37448 | tf_op jit(solution)/shard_map/ppermute | solution.py:21
  108.8 0.4 reverse.2
  109.3 1.0 collective-permute-done.20
  111.5 0.8 add_multiply_fusion.1
  112.3 0.5 add_multiply_fusion.3
  113.5 0.4 pad_maximum_fusion.3
  114.0 0.5 add_multiply_fusion
  116.0 1.0 fusion.86
  (110 shorter events, 11.6 us)
Async XLA Ops:
  0.6 0.9 copy-start.8
  1.6 6.0 %copy-start.9 = (s32[16,128]{1,0:T(8,128)S(1)}, s32[16,128]{1,0:T(8,128)}, u32[]{:S(2)}) copy-start(s32[16,128]{1,0:T(8,128)} %param.13) | copy-start | bytes 24580
  1.6 6.0 %copy-start.10 = (s32[16,128]{1,0:T(8,128)S(1)}, s32[16,128]{1,0:T(8,128)}, u32[]{:S(2)}) copy-start(s32[16,128]{1,0:T(8,128)} %param.12) | copy-start | bytes 24580
  1.6 6.0 %copy-start.4 = (f32[12,16,128]{2,1,0:T(8,128)S(1)}, f32[12,16,128]{2,1,0:T(8,128)}, u32[]{:S(2)}) copy-start(f32[12,16,128]{2,1,0:T(8,128)} %param.10) | copy-start | bytes 294916
  1.6 6.0 %copy-start.5 = (f32[12,16,128]{2,1,0:T(8,128)S(1)}, f32[12,16,128]{2,1,0:T(8,128)}, u32[]{:S(2)}) copy-start(f32[12,16,128]{2,1,0:T(8,128)} %param.9) | copy-start | bytes 294916
  1.8 8.5 %collective-permute-start = (f32[24,16,3]{2,1,0:T(8,128)S(1)}, f32[24,16,3]{2,1,0:T(8,128)S(1)}, u32[]{:S(2)}, u32[]{:S(2)}) collective-permute-start(f32[24,16,3]{2,1,0:T(8,128)S(1)} %get-tuple-element.155), channel_id=1, source_target_pairs={{0,8},{8,16},{16,24},{24,32},{32,40},{40,48},{48,56},{56,64},{64,7... | collective-permute-start | bytes 13832 | tf_op jit(solution)/shard_map/ppermute | solution.py:21
  1.9 8.4 %collective-permute-start.1 = (f32[24,16,3]{2,1,0:T(8,128)S(1)}, f32[24,16,3]{2,1,0:T(8,128)S(1)}, u32[]{:S(2)}, u32[]{:S(2)}) collective-permute-start(f32[24,16,3]{2,1,0:T(8,128)S(1)} %get-tuple-element.156), channel_id=1, source_target_pairs={{8,0},{16,8},{24,16},{32,24},{40,32},{48,40},{56,48},{64,56},{72,6... | collective-permute-start | bytes 13832 | tf_op jit(solution)/shard_map/ppermute | solution.py:24
  10.3 46.2 %copy-start = (f32[24,16,3]{2,1,0:T(8,128)}, f32[24,16,3]{2,1,0:T(8,128)S(1)}, u32[]{:S(2)}) copy-start(f32[24,16,3]{2,1,0:T(8,128)S(1)} %collective-permute-done) | copy-start | bytes 13828
  10.3 46.2 %copy-start.2 = (f32[24,16,3]{2,1,0:T(8,128)}, f32[24,16,3]{2,1,0:T(8,128)S(1)}, u32[]{:S(2)}) copy-start(f32[24,16,3]{2,1,0:T(8,128)S(1)} %collective-permute-done.1) | copy-start | bytes 13828
  10.5 5.4 %collective-permute-start.3 = (f32[24,3,134]{2,1,0:T(4,128)S(1)}, f32[24,3,134]{2,1,0:T(4,128)S(1)}, u32[]{:S(2)}, u32[]{:S(2)}) collective-permute-start(f32[24,3,134]{2,1,0:T(4,128)S(1)} %get-tuple-element.98), channel_id=1, source_target_pairs={{0,8},{8,0},{16,24},{24,16},{32,40},{40,32},{48,56},{56,48},{64,72... | collective-permute-start | bytes 115784 | tf_op jit(solution)/shard_map/ppermute | solution.py:30
  10.7 8.4 %collective-permute-start.10 = (f32[25,16,4]{2,1,0:T(8,128)S(1)}, f32[25,16,4]{2,1,0:T(8,128)S(1)}, u32[]{:S(2)}, u32[]{:S(2)}) collective-permute-start(f32[25,16,4]{2,1,0:T(8,128)S(1)} %get-tuple-element.152), channel_id=1, source_target_pairs={{8,0},{16,8},{24,16},{32,24},{40,32},{48,40},{56,48},{64,56},{72,6... | collective-permute-start | bytes 19208 | tf_op jit(solution)/shard_map/ppermute | solution.py:24
  15.8 8.5 %collective-permute-start.9 = (f32[25,16,4]{2,1,0:T(8,128)S(1)}, f32[25,16,4]{2,1,0:T(8,128)S(1)}, u32[]{:S(2)}, u32[]{:S(2)}) collective-permute-start(f32[25,16,4]{2,1,0:T(8,128)S(1)} %get-tuple-element.151), channel_id=1, source_target_pairs={{0,8},{8,16},{16,24},{24,32},{32,40},{40,48},{48,56},{56,64},{64,7... | collective-permute-start | bytes 19208 | tf_op jit(solution)/shard_map/ppermute | solution.py:21
  15.8 8.8 %collective-permute-start.4 = (f32[24,3,134]{2,1,0:T(4,128)S(1)}, f32[24,3,134]{2,1,0:T(4,128)S(1)}, u32[]{:S(2)}, u32[]{:S(2)}) collective-permute-start(f32[24,3,134]{2,1,0:T(4,128)S(1)} %collective-permute-done.3), channel_id=1, source_target_pairs={{0,16},{8,24},{16,0},{24,8},{32,48},{40,56},{48,32},{56,40},{64,80... | collective-permute-start | bytes 115784 | tf_op jit(solution)/shard_map/ppermute | solution.py:30
  24.6 1.4 %collective-permute-start.12 = (f32[25,4,136]{2,1,0:T(4,128)S(1)}, f32[25,4,136]{2,1,0:T(4,128)S(1)}, u32[]{:S(2)}, u32[]{:S(2)}) collective-permute-start(f32[25,4,136]{2,1,0:T(4,128)S(1)} %get-tuple-element.81), channel_id=1, source_target_pairs={{0,8},{8,0},{16,24},{24,16},{32,40},{40,32},{48,56},{56,48},{64,72... | collective-permute-start | bytes 163208 | tf_op jit(solution)/shard_map/ppermute | solution.py:30
  24.7 7.2 %collective-permute-start.5 = (f32[24,3,134]{2,1,0:T(4,128)S(1)}, f32[24,3,134]{2,1,0:T(4,128)S(1)}, u32[]{:S(2)}, u32[]{:S(2)}) collective-permute-start(f32[24,3,134]{2,1,0:T(4,128)S(1)} %collective-permute-done.4), channel_id=1, source_target_pairs={{0,32},{8,40},{16,48},{24,56},{32,0},{40,8},{48,16},{56,24},{64,96... | collective-permute-start | bytes 115784 | tf_op jit(solution)/shard_map/ppermute | solution.py:30
  26.0 7.9 %collective-permute-start.13 = (f32[25,4,136]{2,1,0:T(4,128)S(1)}, f32[25,4,136]{2,1,0:T(4,128)S(1)}, u32[]{:S(2)}, u32[]{:S(2)}) collective-permute-start(f32[25,4,136]{2,1,0:T(4,128)S(1)} %collective-permute-done.12), channel_id=1, source_target_pairs={{0,16},{8,24},{16,0},{24,8},{32,48},{40,56},{48,32},{56,40},{64,80... | collective-permute-start | bytes 163208 | tf_op jit(solution)/shard_map/ppermute | solution.py:30
  31.9 5.4 %collective-permute-start.6 = (f32[24,3,134]{2,1,0:T(4,128)S(1)}, f32[24,3,134]{2,1,0:T(4,128)S(1)}, u32[]{:S(2)}, u32[]{:S(2)}) collective-permute-start(f32[24,3,134]{2,1,0:T(4,128)S(1)} %collective-permute-done.5), channel_id=1, source_target_pairs={{0,64},{8,72},{16,80},{24,88},{32,96},{40,104},{48,112},{56,120},{... | collective-permute-start | bytes 115784 | tf_op jit(solution)/shard_map/ppermute | solution.py:30
  31.9 16.8 %collective-permute-start.8 = (f32[24,3,134]{2,1,0:T(4,128)S(1)}, f32[24,3,134]{2,1,0:T(4,128)S(1)}, u32[]{:S(2)}, u32[]{:S(2)}) collective-permute-start(f32[24,3,134]{2,1,0:T(4,128)S(1)} %get-tuple-element.97), channel_id=1, source_target_pairs={{1,0},{2,1},{3,2},{4,3},{5,4},{6,5},{7,6},{9,8},{10,9},{11,10},{12... | collective-permute-start | bytes 115784 | tf_op jit(solution)/shard_map/ppermute | solution.py:24
  33.9 10.6 %collective-permute-start.14 = (f32[25,4,136]{2,1,0:T(4,128)S(1)}, f32[25,4,136]{2,1,0:T(4,128)S(1)}, u32[]{:S(2)}, u32[]{:S(2)}) collective-permute-start(f32[25,4,136]{2,1,0:T(4,128)S(1)} %collective-permute-done.13), channel_id=1, source_target_pairs={{0,32},{8,40},{16,48},{24,56},{32,0},{40,8},{48,16},{56,24},{64,96... | collective-permute-start | bytes 163208 | tf_op jit(solution)/shard_map/ppermute | solution.py:30
  37.3 10.9 %collective-permute-start.7 = (f32[24,3,134]{2,1,0:T(4,128)S(1)}, f32[24,3,134]{2,1,0:T(4,128)S(1)}, u32[]{:S(2)}, u32[]{:S(2)}) collective-permute-start(f32[24,3,134]{2,1,0:T(4,128)S(1)} %collective-permute-done.6), channel_id=1, source_target_pairs={{0,128},{8,136},{16,144},{24,152},{32,160},{40,168},{48,176},{56,1... | collective-permute-start | bytes 115784 | tf_op jit(solution)/shard_map/ppermute | solution.py:30
  37.3 19.2 %collective-permute-start.2 = (f32[24,3,134]{2,1,0:T(4,128)S(1)}, f32[24,3,134]{2,1,0:T(4,128)S(1)}, u32[]{:S(2)}, u32[]{:S(2)}) collective-permute-start(f32[24,3,134]{2,1,0:T(4,128)S(1)} %get-tuple-element.98), channel_id=1, source_target_pairs={{0,1},{1,2},{2,3},{3,4},{4,5},{5,6},{6,7},{8,9},{9,10},{10,11},{11... | collective-permute-start | bytes 115784 | tf_op jit(solution)/shard_map/ppermute | solution.py:21
  42.3 17.9 %collective-permute-start.11 = (f32[25,4,136]{2,1,0:T(4,128)S(1)}, f32[25,4,136]{2,1,0:T(4,128)S(1)}, u32[]{:S(2)}, u32[]{:S(2)}) collective-permute-start(f32[25,4,136]{2,1,0:T(4,128)S(1)} %get-tuple-element.81), channel_id=1, source_target_pairs={{0,1},{1,2},{2,3},{3,4},{4,5},{5,6},{6,7},{8,9},{9,10},{10,11},{11... | collective-permute-start | bytes 163208 | tf_op jit(solution)/shard_map/ppermute | solution.py:21
  44.5 15.3 %collective-permute-start.17 = (f32[25,4,136]{2,1,0:T(4,128)S(1)}, f32[25,4,136]{2,1,0:T(4,128)S(1)}, u32[]{:S(2)}, u32[]{:S(2)}) collective-permute-start(f32[25,4,136]{2,1,0:T(4,128)S(1)} %get-tuple-element.82), channel_id=1, source_target_pairs={{1,0},{2,1},{3,2},{4,3},{5,4},{6,5},{7,6},{9,8},{10,9},{11,10},{12... | collective-permute-start | bytes 163208 | tf_op jit(solution)/shard_map/ppermute | solution.py:24
  48.2 5.1 %collective-permute-start.15 = (f32[25,4,136]{2,1,0:T(4,128)S(1)}, f32[25,4,136]{2,1,0:T(4,128)S(1)}, u32[]{:S(2)}, u32[]{:S(2)}) collective-permute-start(f32[25,4,136]{2,1,0:T(4,128)S(1)} %collective-permute-done.14), channel_id=1, source_target_pairs={{0,64},{8,72},{16,80},{24,88},{32,96},{40,104},{48,112},{56,120},{... | collective-permute-start | bytes 163208 | tf_op jit(solution)/shard_map/ppermute | solution.py:30
  53.3 6.2 %collective-permute-start.16 = (f32[25,4,136]{2,1,0:T(4,128)S(1)}, f32[25,4,136]{2,1,0:T(4,128)S(1)}, u32[]{:S(2)}, u32[]{:S(2)}) collective-permute-start(f32[25,4,136]{2,1,0:T(4,128)S(1)} %collective-permute-done.15), channel_id=1, source_target_pairs={{0,128},{8,136},{16,144},{24,152},{32,160},{40,168},{48,176},{56,1... | collective-permute-start | bytes 163208 | tf_op jit(solution)/shard_map/ppermute | solution.py:30
  56.5 0.6 copy-start.6
  59.4 0.7 copy-start.11
  65.4 0.9 copy-start.1
  65.4 1.0 copy-start.3
  65.4 1.1 copy-start.7
  76.6 8.7 %collective-permute-start.18 = (f32[24,16,1]{2,1,0:T(8,128)S(1)}, f32[24,16,1]{2,1,0:T(8,128)S(1)}, u32[]{:S(2)}, u32[]{:S(2)}) collective-permute-start(f32[24,16,1]{2,1,0:T(8,128)S(1)} %get-tuple-element.153), channel_id=1, source_target_pairs={{0,8},{8,16},{16,24},{24,32},{32,40},{40,48},{48,56},{56,64},{64,7... | collective-permute-start | bytes 4616 | tf_op jit(solution)/shard_map/ppermute | solution.py:21
  76.9 8.4 %collective-permute-start.19 = (f32[24,16,1]{2,1,0:T(8,128)S(1)}, f32[24,16,1]{2,1,0:T(8,128)S(1)}, u32[]{:S(2)}, u32[]{:S(2)}) collective-permute-start(f32[24,16,1]{2,1,0:T(8,128)S(1)} %get-tuple-element.154), channel_id=1, source_target_pairs={{8,0},{16,8},{24,16},{32,24},{40,32},{48,40},{56,48},{64,56},{72,6... | collective-permute-start | bytes 4616 | tf_op jit(solution)/shard_map/ppermute | solution.py:24
  85.5 1.3 %collective-permute-start.21 = (f32[24,1,130]{2,1,0:T(1,128)S(1)}, f32[24,1,130]{2,1,0:T(1,128)S(1)}, u32[]{:S(2)}, u32[]{:S(2)}) collective-permute-start(f32[24,1,130]{2,1,0:T(1,128)S(1)} %get-tuple-element.94), channel_id=1, source_target_pairs={{0,8},{8,0},{16,24},{24,16},{32,40},{40,32},{48,56},{56,48},{64,72... | collective-permute-start | bytes 37448 | tf_op jit(solution)/shard_map/ppermute | solution.py:30
  86.8 3.8 %collective-permute-start.22 = (f32[24,1,130]{2,1,0:T(1,128)S(1)}, f32[24,1,130]{2,1,0:T(1,128)S(1)}, u32[]{:S(2)}, u32[]{:S(2)}) collective-permute-start(f32[24,1,130]{2,1,0:T(1,128)S(1)} %collective-permute-done.21), channel_id=1, source_target_pairs={{0,16},{8,24},{16,0},{24,8},{32,48},{40,56},{48,32},{56,40},{64,80... | collective-permute-start | bytes 37448 | tf_op jit(solution)/shard_map/ppermute | solution.py:30
  90.6 5.3 %collective-permute-start.23 = (f32[24,1,130]{2,1,0:T(1,128)S(1)}, f32[24,1,130]{2,1,0:T(1,128)S(1)}, u32[]{:S(2)}, u32[]{:S(2)}) collective-permute-start(f32[24,1,130]{2,1,0:T(1,128)S(1)} %collective-permute-done.22), channel_id=1, source_target_pairs={{0,32},{8,40},{16,48},{24,56},{32,0},{40,8},{48,16},{56,24},{64,96... | collective-permute-start | bytes 37448 | tf_op jit(solution)/shard_map/ppermute | solution.py:30
  96.0 3.8 %collective-permute-start.24 = (f32[24,1,130]{2,1,0:T(1,128)S(1)}, f32[24,1,130]{2,1,0:T(1,128)S(1)}, u32[]{:S(2)}, u32[]{:S(2)}) collective-permute-start(f32[24,1,130]{2,1,0:T(1,128)S(1)} %collective-permute-done.23), channel_id=1, source_target_pairs={{0,64},{8,72},{16,80},{24,88},{32,96},{40,104},{48,112},{56,120},{... | collective-permute-start | bytes 37448 | tf_op jit(solution)/shard_map/ppermute | solution.py:30
  99.8 9.0 %collective-permute-start.25 = (f32[24,1,130]{2,1,0:T(1,128)S(1)}, f32[24,1,130]{2,1,0:T(1,128)S(1)}, u32[]{:S(2)}, u32[]{:S(2)}) collective-permute-start(f32[24,1,130]{2,1,0:T(1,128)S(1)} %collective-permute-done.24), channel_id=1, source_target_pairs={{0,128},{8,136},{16,144},{24,152},{32,160},{40,168},{48,176},{56,1... | collective-permute-start | bytes 37448 | tf_op jit(solution)/shard_map/ppermute | solution.py:30
  101.8 7.5 %collective-permute-start.26 = (f32[24,1,130]{2,1,0:T(1,128)S(1)}, f32[24,1,130]{2,1,0:T(1,128)S(1)}, u32[]{:S(2)}, u32[]{:S(2)}) collective-permute-start(f32[24,1,130]{2,1,0:T(1,128)S(1)} %get-tuple-element.93), channel_id=1, source_target_pairs={{1,0},{2,1},{3,2},{4,3},{5,4},{6,5},{7,6},{9,8},{10,9},{11,10},{12... | collective-permute-start | bytes 37448 | tf_op jit(solution)/shard_map/ppermute | solution.py:24
  103.7 6.6 %collective-permute-start.20 = (f32[24,1,130]{2,1,0:T(1,128)S(1)}, f32[24,1,130]{2,1,0:T(1,128)S(1)}, u32[]{:S(2)}, u32[]{:S(2)}) collective-permute-start(f32[24,1,130]{2,1,0:T(1,128)S(1)} %get-tuple-element.94), channel_id=1, source_target_pairs={{0,1},{1,2},{2,3},{3,4},{4,5},{5,6},{6,7},{8,9},{9,10},{10,11},{11... | collective-permute-start | bytes 37448 | tf_op jit(solution)/shard_map/ppermute | solution.py:21
where the time goes:
time: 118 us; the launch traced here: 117 us
  waiting for transfers between devices  46.1 us (39%)
  starting transfers between devices  41.9 us (36%)
  other arithmetic  19.1 us (16%)
  local copies, waits for them, and re-layouts  7.86 us (7%)
  between operations  1.97 us (2%)
    ppermute x15, waiting for transfers between devices, partner(): lax.ppermute(array, axis, [(i, i ^ 1 << apart) for i in range(lax.axis_si...  30.6 us
    ppermute x6, starting transfers between devices, with_halo(): lax.ppermute(lax.slice_in_dim(block, 0, width, axis=dim), axis, backward)  22.8 us
    ppermute x6, starting transfers between devices, with_halo(): lax.ppermute(lax.slice_in_dim(block, block.shape[dim] - width, None, axis...  12.7 us
    ppermute x6, waiting for transfers between devices, with_halo(): lax.ppermute(lax.slice_in_dim(block, block.shape[dim] - width, None, axis...  12.2 us
    ppermute x15, starting transfers between devices, partner(): lax.ppermute(array, axis, [(i, i ^ 1 << apart) for i in range(lax.axis_si...  6.39 us
    select_n x4, other arithmetic, limit_ratio(): jnp.where(supply > headroom, headroom / jnp.where(supply > headroom, supp...  4.24 us
    unnamed x28, local copies, waits for them, and re-layouts  3.62 us
    ppermute x6, waiting for transfers between devices, with_halo(): lax.ppermute(lax.slice_in_dim(block, 0, width, axis=dim), axis, backward)  3.27 us
  transfers between devices with their start and end apart: 27, of which 14 were waited for; matrix products, arithmetic and copies ran while one was open for 2% of the time, Pallas kernels for 0%

commit v1 on v0

v1 whole, which is shorter than its diff:
```python
import functools

import jax
import jax.numpy as jnp
from jax import lax
from jax.experimental import pallas as pl
from jax.experimental.pallas import tpu as pltpu
from jax.sharding import PartitionSpec as P

time_step = 0.5
diffusivity = 0.1
strat_floor = 0.5
slope_limit = 2.0
thermal_coef = 0.2
haline_coef = 0.8

MESH = pl.DeviceIdType.MESH
INF = float("inf")
TINY = 1e-37
FACE_SCALE = 0.25 * time_step
DIFF_SCALE = 0.25 * time_step * diffusivity

EAST, WEST, NORTH, SOUTH, NE, NW, SE, SW = range(8)


def east_of(x):
    return pltpu.roll(x, x.shape[1] - 1, 1)


def west_of(x):
    return pltpu.roll(x, 1, 1)


def south_of(x):
    return pltpu.roll(x, 1, 0)


def stage_flux(z, wins):
    nk = z["u"].shape[0]
    stat = []
    for r0, n, _, _ in wins:
        f = z["f"][r0 : r0 + n, :]
        f_e = jnp.minimum(f, east_of(f))
        f_n = jnp.minimum(f, z["f"][r0 + 1 : r0 + 1 + n, :])
        stat.append((f, f_e, f_n))

    def body(i, carry):
        k = nk - 1 - i
        kk = k.astype(jnp.float32)
        up_k = jnp.maximum(k - 1, 0)
        out = []
        for (r0, n, lo, hi), (f, f_e, f_n), (w_old, bottoms) in zip(wins, stat, carry):
            u = z["u"][k, r0 : r0 + n, :]
            u_e = jnp.where(kk < f_e, FACE_SCALE * (u + east_of(u)), 0.0)
            v = z["v"][k, r0 : r0 + n, :]
            v_n = jnp.where(kk < f_n, FACE_SCALE * (v + z["v"][k, r0 + 1 : r0 + 1 + n, :]), 0.0)
            w = w_old - (u_e - west_of(u_e) + v_n - south_of(v_n))
            abs_u, abs_v, abs_w = jnp.abs(u_e), jnp.abs(v_n), jnp.abs(w)
            wet = kk < f
            tops = []
            for m, t in enumerate(z["t"]):
                c = t[k, r0 : r0 + n, :]
                e = east_of(c)
                nn = t[k, r0 + 1 : r0 + 1 + n, :]
                up = t[up_k, r0 : r0 + n, :]
                a_e = abs_u * (e - c)
                l_e = u_e * (c + e) - a_e
                a_n = abs_v * (nn - c)
                l_n = v_n * (c + nn) - a_n
                a_t = abs_w * (up - c)
                l_t = w * (c + up) - a_t
                low = c - ((l_e - west_of(l_e)) + (l_n - south_of(l_n)) + (l_t - bottoms[m]))
                low = jnp.where(wet, low, 0.0)
                big = jnp.where(wet, jnp.maximum(c, low), -INF)
                small = jnp.where(wet, jnp.minimum(c, low), INF)
                for name, val in (("ax", a_e), ("ay", a_n), ("az", a_t), ("low", low), ("mx", big), ("mn", small)):
                    z[name][m][k, r0 + lo : r0 + hi, :] = val[lo:hi]
                tops.append(l_t)
            out.append((w, tuple(tops)))
        return tuple(out)

    zero = [jnp.zeros((n, 128), jnp.float32) for _, n, _, _ in wins]
    lax.fori_loop(0, nk, body, tuple((x, tuple(x for _ in z["t"])) for x in zero))


def stage_ratio(z, wins):
    nk = z["u"].shape[0]

    def body(i, carry):
        k = nk - 1 - i
        up_k, down_k = jnp.maximum(k - 1, 0), jnp.minimum(k + 1, nk - 1)
        out = []
        for (r0, n, lo, hi), bottoms in zip(wins, carry):
            tops = []
            for m in range(len(z["t"])):
                def near(ref, pick):
                    c = ref[k, r0 : r0 + n, :]
                    horizontal = pick(pick(east_of(c), west_of(c)), pick(ref[k, r0 + 1 : r0 + 1 + n, :], ref[k, r0 - 1 : r0 - 1 + n, :]))
                    return pick(pick(c, horizontal), pick(ref[up_k, r0 : r0 + n, :], ref[down_k, r0 : r0 + n, :]))

                big, small = near(z["mx"][m], jnp.maximum), near(z["mn"][m], jnp.minimum)
                low = z["low"][m][k, r0 : r0 + n, :]
                a_e = z["ax"][m][k, r0 : r0 + n, :]
                a_w = west_of(a_e)
                a_n = z["ay"][m][k, r0 : r0 + n, :]
                a_s = z["ay"][m][k, r0 - 1 : r0 - 1 + n, :]
                a_t, a_b = z["az"][m][k, r0 : r0 + n, :], bottoms[m]
                p_in, p_out = 0.0, 0.0
                for inward, outward in ((a_w, a_e), (a_s, a_n), (a_b, a_t)):
                    p_in = p_in + (jnp.maximum(inward, 0.0) - jnp.minimum(outward, 0.0))
                    p_out = p_out + (jnp.maximum(outward, 0.0) - jnp.minimum(inward, 0.0))
                r_in = jnp.clip((big - low) * pl.reciprocal(jnp.maximum(p_in, TINY)), 0.0, 1.0)
                r_out = jnp.clip((low - small) * pl.reciprocal(jnp.maximum(p_out, TINY)), 0.0, 1.0)
                z["rin"][m][k, r0 + lo : r0 + hi, :] = r_in[lo:hi]
                z["rout"][m][k, r0 + lo : r0 + hi, :] = r_out[lo:hi]
                tops.append(a_t)
            out.append(tuple(tops))
        return tuple(out)

    lax.fori_loop(0, nk, body, tuple(tuple(jnp.zeros((n, 128), jnp.float32) for _ in z["t"]) for _, n, _, _ in wins))


def stage_limit(z, wins):
    nk = z["u"].shape[0]
    stat = [z["f"][r0 : r0 + n, :] for r0, n, _, _ in wins]

    def body(i, carry):
        k = nk - 1 - i
        kk = k.astype(jnp.float32)
        up_k = jnp.maximum(k - 1, 0)
        out = []
        for (r0, n, lo, hi), f, bottoms in zip(wins, stat, carry):
            tops = []
            for m in range(len(z["t"])):
                r_in, r_out = z["rin"][m][k, r0 : r0 + n, :], z["rout"][m][k, r0 : r0 + n, :]

                def limited(anti, far_in, far_out):
                    return anti * jnp.where(anti >= 0, jnp.minimum(far_in, r_out), jnp.minimum(r_in, far_out))

                f_e = limited(z["ax"][m][k, r0 : r0 + n, :], east_of(r_in), east_of(r_out))
                f_n = limited(
                    z["ay"][m][k, r0 : r0 + n, :],
                    z["rin"][m][k, r0 + 1 : r0 + 1 + n, :],
                    z["rout"][m][k, r0 + 1 : r0 + 1 + n, :],
                )
                f_t = limited(
                    z["az"][m][k, r0 : r0 + n, :],
                    z["rin"][m][up_k, r0 : r0 + n, :],
                    z["rout"][m][up_k, r0 : r0 + n, :],
                )
                low = z["low"][m][k, r0 : r0 + n, :]
                new = low - ((f_e - west_of(f_e)) + (f_n - south_of(f_n)) + (f_t - bottoms[m]))
                new = jnp.where(kk < f, new, 0.0)
                z["adv"][m][k, r0 + lo : r0 + hi, :] = new[lo:hi]
                tops.append(f_t)
            out.append(tuple(tops))
        return tuple(out)

    lax.fori_loop(0, nk, body, tuple(tuple(jnp.zeros((n, 128), jnp.float32) for _ in z["t"]) for _, n, _, _ in wins))


def clip_slope(x):
    return jnp.clip(x, -slope_limit, slope_limit)


def stage_diffuse(z, wins, emit):
    nk = z["u"].shape[0]
    dens = z["density"]
    nt = len(z["t"])
    stat = []
    for r0, n, _, _ in wins:
        f = z["f"][r0 : r0 + n, :]
        far_e, far_n = east_of(f), z["f"][r0 + 1 : r0 + 1 + n, :]
        stat.append((f, far_e, far_n, jnp.minimum(f, far_e), jnp.minimum(f, far_n)))

    def inverse(grads):
        return pl.reciprocal(jnp.maximum(-dens(grads), strat_floor))

    def body(i, carry):
        k = nk - 1 - i
        kk = k.astype(jnp.float32)
        up_k = jnp.maximum(k - 1, 0)
        below_k = jnp.minimum(k + 1, nk - 1)
        not_top = (k >= 1).astype(jnp.float32)
        out = []
        for wi, ((r0, n, _, _), (f, far_e, far_n, f_e, f_n), old) in enumerate(zip(wins, stat, carry)):
            here = [a[k, r0 : r0 + n, :] for a in z["adv"]]
            north = [a[k, r0 + 1 : r0 + 1 + n, :] for a in z["adv"]]
            gz = [jnp.where(kk < f, a[up_k, r0 : r0 + n, :] - c, 0.0) for a, c in zip(z["adv"], here)]
            gz_n = [jnp.where(kk < far_n, a[up_k, r0 + 1 : r0 + 1 + n, :] - c, 0.0) for a, c in zip(z["adv"], north)]
            gz_e = [east_of(g) for g in gz]
            inv, inv_n = inverse(gz), inverse(gz_n)
            inv_e = east_of(inv)
            gx = [jnp.where(kk < f_e, east_of(c) - c, 0.0) for c in here]
            gy = [jnp.where(kk < f_n, b - c, 0.0) for b, c in zip(north, here)]
            rx, ry = dens(gx), dens(gy)
            (o_inv, o_inv_e, o_inv_n, o_gz, o_gz_e, o_gz_n, o_part, o_top) = old
            low_here, low_e, low_n = kk + 1.0 < f, kk + 1.0 < far_e, kk + 1.0 < far_n
            s_x = [clip_slope(rx * q) for q in (inv, inv_e, o_inv, o_inv_e)]
            s_y = [clip_slope(ry * q) for q in (inv, inv_n, o_inv, o_inv_n)]
            parts, tops = [], []
            for m in range(nt):
                gx_top, gy_top = gx[m] * not_top, gy[m] * not_top
                hx = (
                    gx_top + s_x[0] * gz[m],
                    gx_top + s_x[1] * gz_e[m],
                    jnp.where(low_here, gx[m], 0.0) + s_x[2] * o_gz[m],
                    jnp.where(low_e, gx[m], 0.0) + s_x[3] * o_gz_e[m],
                )
                hy = (
                    gy_top + s_y[0] * gz[m],
                    gy_top + s_y[1] * gz_n[m],
                    jnp.where(low_here, gy[m], 0.0) + s_y[2] * o_gz[m],
                    jnp.where(low_n, gy[m], 0.0) + s_y[3] * o_gz_n[m],
                )
                flux_e = (hx[0] + hx[1]) + (hx[2] + hx[3])
                flux_n = (hy[0] + hy[1]) + (hy[2] + hy[3])
                top = (s_x[0] * hx[0] + west_of(s_x[1] * hx[1])) + (s_y[0] * hy[0] + south_of(s_y[1] * hy[1]))
                bottom = (s_x[2] * hx[2] + west_of(s_x[3] * hx[3])) + (s_y[2] * hy[2] + south_of(s_y[3] * hy[3]))
                rise = o_top[m] + bottom
                done = jnp.where(kk + 1.0 < f, o_part[m] + DIFF_SCALE * rise, 0.0)
                emit(below_k, wi, m, done)
                parts.append(here[m] + DIFF_SCALE * ((flux_e - west_of(flux_e)) + (flux_n - south_of(flux_n)) - rise))
                tops.append(top)
            out.append((inv, inv_e, inv_n, tuple(gz), tuple(gz_e), tuple(gz_n), tuple(parts), tuple(tops)))
        return tuple(out)

    start = []
    for _, n, _, _ in wins:
        x = jnp.zeros((n, 128), jnp.float32)
        xs = tuple(x for _ in range(nt))
        start.append((x, x, x, xs, xs, xs, xs, xs))
    last = lax.fori_loop(0, nk, body, tuple(start))
    for wi, ((f, *_), old) in enumerate(zip(stat, last)):
        for m in range(nt):
            emit(0, wi, m, jnp.where(0.0 < f, old[6][m] + DIFF_SCALE * old[7][m], 0.0))


def lane_iota(rows):
    return lax.broadcasted_iota(jnp.int32, (rows, 128), 1)


def kernel(
    t_hbm, s_hbm, u_hbm, v_hbm, flag_ref, point_ref, count_ref,
    t_out, s_out,
    tr, u, v, floor, low, mx, mn, ax, ay, az, rin, rout, adv,
    e_tr, e_u, e_v, e_floor, e_low, e_mx, e_mn, e_ax, e_ay, e_az, e_rin, e_rout, e_adv, e_res,
    row_out, row_in, strip_out, fold_out, strip_in, corner_in,
    load_sem, send_sem, recv_sem,
):
    n_lon, n_lat = lax.axis_size("lon"), lax.axis_size("lat")
    lon, lat = lax.axis_index("lon"), lax.axis_index("lat")
    nk = u.shape[0]
    half = nk // 2
    east, west = lax.rem(lon + 1, n_lon), lax.rem(lon + n_lon - 1, n_lon)
    at_north, at_south = lat == n_lat - 1, lat == 0
    fold_mid = n_lon - 1 - lon
    fold_ne = lax.rem(2 * n_lon - 2 - lon, n_lon)
    fold_nw = lax.rem(n_lon - lon, n_lon)

    side = [(EAST, (east, lat)), (WEST, (west, lat))]
    north = [(NORTH, (lon, lat + 1)), (NE, (east, lat + 1)), (NW, (west, lat + 1))]
    south = [(SOUTH, (lon, lat - 1)), (SE, (east, lat - 1)), (SW, (west, lat - 1))]
    folded = [(NORTH, (fold_mid, lat)), (NE, (fold_ne, lat)), (NW, (fold_nw, lat))]
    ne_self, nw_self = fold_ne == lon, fold_nw == lon
    not_self = {NORTH: True, NE: jnp.logical_not(ne_self), NW: jnp.logical_not(nw_self)}

    barrier = pltpu.get_barrier_semaphore()

    def greet(where):
        pl.semaphore_signal(barrier, inc=1, device_id=where, device_id_type=MESH)

    for _, where in side:
        greet(where)

    @pl.when(jnp.logical_not(at_south))
    def _():
        for _, where in south:
            greet(where)

    @pl.when(jnp.logical_not(at_north))
    def _():
        for _, where in north:
            greet(where)

    @pl.when(at_north)
    def _():
        greet(folded[0][1])

        @pl.when(jnp.logical_not(ne_self))
        def _():
            greet(folded[1][1])

        @pl.when(jnp.logical_not(nw_self))
        def _():
            greet(folded[2][1])

    loads = [
        pltpu.make_async_copy(src, dst.at[:, 8:24, :], load_sem.at[i])
        for i, (src, dst) in enumerate(((t_hbm, tr.at[0]), (s_hbm, tr.at[1]), (u_hbm, u), (v_hbm, v)))
    ]
    for copy in loads:
        copy.start()
    floor[8:24, :] = (count_ref[...] * point_ref[...] * flag_ref[...]).astype(jnp.float32)
    for copy in loads:
        copy.wait()

    fields = ((tr.at[0], tr.at[1]), (u, v))
    for g, (a, b) in enumerate(fields):
        for k in range(nk):
            row_out[1, g * nk + k, 0:4, :] = a[k, 8:12, :]
            row_out[1, g * nk + k, 4:8, :] = b[k, 8:12, :]
    row_out[1, 2 * nk, 0:4, :] = floor[8:12, :]

    @pl.when(jnp.logical_not(at_north))
    def _():
        for g, (a, b) in enumerate(fields):
            for k in range(nk):
                row_out[0, g * nk + k, 0:4, :] = a[k, 20:24, :]
                row_out[0, g * nk + k, 4:8, :] = b[k, 20:24, :]
        row_out[0, 2 * nk, 0:4, :] = floor[20:24, :]

    lane8, sub8 = lane_iota(8), lax.broadcasted_iota(jnp.int32, (8, 128), 0)

    @pl.when(at_north)
    def _():
        def turned(x):
            x = jnp.take_along_axis(x, 127 - lane8, axis=1)
            return jnp.take_along_axis(x, 7 - sub8, axis=0)

        for g, (a, b) in enumerate(fields):
            sign = 1.0 if g == 0 else -1.0
            for k in range(nk):
                row_out[0, g * nk + k, 0:4, :] = sign * turned(a[k, 16:24, :])[0:4]
                row_out[0, g * nk + k, 4:8, :] = sign * turned(b[k, 16:24, :])[0:4]
        row_out[0, 2 * nk, 0:4, :] = turned(floor[16:24, :])[0:4]

    p = lax.rem(lane8, 64)
    shift = jnp.where(p < 12, 116, jnp.where(p < 16, -12, jnp.where(p < 20, 108, -20)))
    strip_idx = lax.rem(p + shift + 128, 128)
    first = lane8 < 64

    def strip_tile(row):
        def gather(x):
            return jnp.take_along_axis(x, strip_idx, axis=1)

        rows = slice(row, row + 8)
        for k in range(nk):
            e_tr[k, rows, :] = jnp.where(first, gather(tr[0, k, rows, :]), gather(tr[1, k, rows, :]))
            e_u[k, rows, :] = gather(u[k, rows, :])
            e_v[k, rows, :] = gather(v[k, rows, :])
        e_floor[rows, :] = gather(floor[rows, :])

    q = lax.rem(lane8, 32)
    q_t = jnp.logical_and(q >= 12, q < 20)
    q_u = jnp.logical_and(q >= 20, q < 28)
    p32 = lax.rem(lane8 + 124, 64) < 32
    for row in (8, 16):
        strip_tile(row)
        rows = slice(row, row + 8)
        for k in range(half):
            def packed(level):
                return jnp.where(
                    q_t, e_tr[level, rows, :],
                    jnp.where(q_u, pltpu.roll(e_u[level, rows, :], 8, 1), pltpu.roll(e_v[level, rows, :], 16, 1)),
                )

            strip_out[k, row - 8 : row, :] = jnp.where(p32, packed(k), pltpu.roll(packed(k + half), 32, 1))
        strip_out[half, row - 8 : row, :] = e_floor[rows, :]

    @pl.when(at_north)
    def _():
        group_idx = lax.rem(lane8 + 7 - 2 * lax.rem(lane8 + 4, 8) + 128, 128)
        sign = jnp.where(q_t, 1.0, -1.0)
        for k in range(half + 1):
            x = jnp.take_along_axis(strip_out[k, 8:16, :], group_idx, axis=1)
            x = jnp.take_along_axis(x, 7 - sub8, axis=0)
            fold_out[k] = x if k == half else x * sign

    n_north = jnp.where(at_north, 3 - ne_self.astype(jnp.int32) - nw_self.astype(jnp.int32), 3)
    pl.semaphore_wait(barrier, 2 + n_north + jnp.where(at_south, 0, 3))

    def send(src, dst, role, slot, where):
        return pltpu.make_async_remote_copy(
            src_ref=src, dst_ref=dst, send_sem=send_sem.at[role], recv_sem=recv_sem.at[slot],
            device_id=where, device_id_type=MESH,
        )

    corner = {NE: 0, NW: 1, SE: 2, SW: 3}

    def to_rows(role, slot, where):
        return send(row_out.at[0 if role == NORTH else 1], row_in.at[0 if slot == NORTH else 1], role, slot, where)

    def to_corner(role, slot, where, fold=False):
        src = fold_out if fold else strip_out.at[:, 8:16, :] if role in (NE, NW) else strip_out.at[:, 0:8, :]
        return send(src, corner_in.at[corner[slot]], role, slot, where)

    side_sends = [
        send(strip_out, strip_in.at[0], WEST, EAST, (west, lat)),
        send(strip_out, strip_in.at[1], EAST, WEST, (east, lat)),
    ]
    north_sends = [
        to_rows(NORTH, SOUTH, north[0][1]),
        to_corner(NE, SW, north[1][1]),
        to_corner(NW, SE, north[2][1]),
    ]
    south_sends = [
        to_rows(SOUTH, NORTH, south[0][1]),
        to_corner(SE, NW, south[1][1]),
        to_corner(SW, NE, south[2][1]),
    ]
    fold_sends = [
        to_rows(NORTH, NORTH, folded[0][1]),
        to_corner(NE, NE, folded[1][1], True),
        to_corner(NW, NW, folded[2][1], True),
    ]
    ne_local = pltpu.make_async_copy(fold_out, corner_in.at[corner[NE]], send_sem.at[NE])
    nw_local = pltpu.make_async_copy(fold_out, corner_in.at[corner[NW]], send_sem.at[NW])

    @pl.when(jnp.logical_not(at_south))
    def _():
        for copy in south_sends:
            copy.start()

    @pl.when(jnp.logical_not(at_north))
    def _():
        for copy in north_sends:
            copy.start()

    @pl.when(at_north)
    def _():
        fold_sends[0].start()
        for copy, local, own in ((fold_sends[1], ne_local, ne_self), (fold_sends[2], nw_local, nw_self)):
            @pl.when(own)
            def _():
                local.start()

            @pl.when(jnp.logical_not(own))
            def _():
                copy.start()

    for copy in side_sends:
        copy.start()

    main = dict(
        t=[tr.at[0], tr.at[1]], u=u, v=v, f=floor,
        density=lambda pair: haline_coef * pair[1] - thermal_coef * pair[0],
    )
    names = dict(low=low, mx=mx, mn=mn, ax=ax, ay=ay, az=az, rin=rin, rout=rout, adv=adv)
    main.update({name: [ref.at[0], ref.at[1]] for name, ref in names.items()})

    outs = (t_out, s_out)

    stage_flux(main, [(8, 16, 0, 16)])
    stage_ratio(main, [(8, 16, 0, 16)])
    stage_limit(main, [(8, 16, 0, 16)])

    def emit_inner(k, wi, m, val):
        outs[m][k, 4:12, :] = val[4:12]

    stage_diffuse(main, [(8, 16, 4, 12)], emit_inner)

    @pl.when(at_south)
    def _():
        row_in[1] = jnp.zeros(row_in.shape[1:], jnp.float32)
        corner_in[corner[SE]] = jnp.zeros(corner_in.shape[1:], jnp.float32)
        corner_in[corner[SW]] = jnp.zeros(corner_in.shape[1:], jnp.float32)

    @pl.when(jnp.logical_not(at_south))
    def _():
        for copy in north_sends:
            copy.wait_recv()
        for copy in south_sends:
            copy.wait_send()

    @pl.when(jnp.logical_not(at_north))
    def _():
        for copy in south_sends:
            copy.wait_recv()
        for copy in north_sends:
            copy.wait_send()

    @pl.when(at_north)
    def _():
        fold_sends[0].wait()
        for copy, local, own in ((fold_sends[1], ne_local, ne_self), (fold_sends[2], nw_local, nw_self)):
            @pl.when(own)
            def _():
                local.wait()

            @pl.when(jnp.logical_not(own))
            def _():
                copy.wait()

    for copy in side_sends:
        copy.wait()

    for slot, row in ((1, 4), (0, 24)):
        for g, (a, b) in enumerate(fields):
            for k in range(nk):
                a[k, row : row + 4, :] = row_in[slot, g * nk + k, 0:4, :]
                b[k, row : row + 4, :] = row_in[slot, g * nk + k, 4:8, :]
        floor[row : row + 4, :] = row_in[slot, 2 * nk, 0:4, :]

    strip_tile(0)
    strip_tile(24)
    halo = jnp.logical_and(p >= 12, p < 20)
    from_east = lax.rem(lane8, 8) >= 4
    for row, east_ref, west_ref, at in (
        (0, corner_in.at[corner[SE]], corner_in.at[corner[SW]], 0),
        (8, strip_in.at[0], strip_in.at[1], 0),
        (16, strip_in.at[0], strip_in.at[1], 8),
        (24, corner_in.at[corner[NE]], corner_in.at[corner[NW]], 0),
    ):
        rows = slice(row, row + 8)
        for k in range(half + 1):
            x = jnp.where(from_east, east_ref[k, at : at + 8, :], west_ref[k, at : at + 8, :])
            if k == half:
                e_floor[rows, :] = jnp.where(halo, x, e_floor[rows, :])
                continue
            for level, y in ((k, x), (k + half, pltpu.roll(x, 96, 1))):
                e_tr[level, rows, :] = jnp.where(halo, y, e_tr[level, rows, :])
                e_u[level, rows, :] = jnp.where(halo, pltpu.roll(y, 120, 1), e_u[level, rows, :])
                e_v[level, rows, :] = jnp.where(halo, pltpu.roll(y, 112, 1), e_v[level, rows, :])

    stage_flux(main, [(4, 8, 1, 5), (20, 8, 3, 7)])
    stage_ratio(main, [(4, 8, 2, 6), (20, 8, 2, 6)])
    stage_limit(main, [(4, 8, 3, 7), (20, 8, 1, 5)])

    def emit_outer(k, wi, m, val):
        if wi == 0:
            outs[m][k, 0:4, :] = val[4:8]
        else:
            outs[m][k, 12:16, :] = val[4:8]

    stage_diffuse(main, [(4, 8, 4, 8), (16, 8, 4, 8)], emit_outer)

    def strip_density(one):
        x = one[0]
        low_half = lane_iota(x.shape[0]) < 64
        own = jnp.where(low_half, -thermal_coef, haline_coef)
        other = jnp.where(low_half, haline_coef, -thermal_coef)
        return own * x + other * pltpu.roll(x, 64, 1)

    strips = dict(t=[e_tr], u=e_u, v=e_v, f=e_floor, density=strip_density)
    names = dict(low=e_low, mx=e_mx, mn=e_mn, ax=e_ax, ay=e_ay, az=e_az, rin=e_rin, rout=e_rout, adv=e_adv)
    strips.update({name: [ref] for name, ref in names.items()})
    stage_flux(strips, [(4, 24, 0, 24)])
    stage_ratio(strips, [(4, 24, 0, 24)])
    stage_limit(strips, [(4, 24, 0, 24)])

    def emit_strip(k, wi, m, val):
        e_res[k] = val[4:20]

    stage_diffuse(strips, [(4, 24, 4, 20)], emit_strip)

    lane16 = lane_iota(16)
    rim = jnp.logical_or(lane16 < 4, lane16 >= 124)
    for m in range(2):
        back = jnp.where(lane16 < 4, lane16 + 20, jnp.where(lane16 >= 124, lane16 - 116, 0)) + 64 * m
        for k in range(nk):
            outs[m][k] = jnp.where(rim, jnp.take_along_axis(e_res[k], back, axis=1), outs[m][k])


def on_device(t, s, u, v, flag, point, count):
    nk = t.shape[0]
    f32 = jnp.float32
    vm = lambda *shape: pltpu.VMEM(shape, f32)
    big = lambda: vm(2, nk, 32, 128)
    one = lambda: vm(nk, 32, 128)
    whole = pl.BlockSpec(memory_space=pltpu.VMEM)
    hbm = pl.BlockSpec(memory_space=pl.ANY)
    return pl.pallas_call(
        kernel,
        out_shape=(jax.ShapeDtypeStruct(t.shape, f32), jax.ShapeDtypeStruct(s.shape, f32)),
        in_specs=[hbm] * 4 + [whole] * 3,
        out_specs=(whole, whole),
        scratch_shapes=[
            big(), one(), one(), vm(32, 128),
            *[big() for _ in range(9)],
            one(), one(), one(), vm(32, 128),
            *[one() for _ in range(9)],
            vm(nk, 16, 128),
            vm(2, 2 * nk + 1, 8, 128), vm(2, 2 * nk + 1, 8, 128),
            vm(nk // 2 + 1, 16, 128), vm(nk // 2 + 1, 8, 128),
            vm(2, nk // 2 + 1, 16, 128), vm(4, nk // 2 + 1, 8, 128),
            pltpu.SemaphoreType.DMA((4,)), pltpu.SemaphoreType.DMA((8,)), pltpu.SemaphoreType.DMA((8,)),
        ],
        compiler_params=pltpu.CompilerParams(
            collective_id=0, has_side_effects=True, vmem_limit_bytes=32 * 1024 * 1024
        ),
    )(t, s, u, v, flag, point, count)


def solution(mesh):
    grid = P(None, "lat", "lon")
    flat = P("lat", "lon")
    return jax.shard_map(
        on_device, mesh=mesh, in_specs=(grid,) * 4 + (flat,) * 3, out_specs=(grid, grid), check_vma=False
    )
```

time: 118 us -> 37.9 us (0.32)
  waiting for transfers between devices: 46.1 us -> 0 us
  starting transfers between devices: 41.9 us -> 0 us
  Pallas kernels: 0 us -> 30 us
  other arithmetic: 19.1 us -> 0 us
  local copies, waits for them, and re-layouts: 7.86 us -> 6.24 us
    ppermute x27 -> x0, waiting for transfers between devices: 46.1 us -> none  [the longest x15 30.6 us: partner(): lax.ppermute(array, axis, [(i, i ^ 1 << apart) for i in range(lax.axis_si...]
    ppermute x27 -> x0, starting transfers between devices: 41.9 us -> none  [the longest x6 22.8 us: with_halo(): lax.ppermute(lax.slice_in_dim(block, 0, width, axis=dim), axis, backward)]
    pallas_call x0 -> x1, Pallas kernels: none -> 30 us  [on_device(): pl.pallas_call(kernel, out_shape=(jax.ShapeDtypeStruct(t.shape, f32), jax...]
    mul x26 -> x0, other arithmetic: 7.76 us -> none  [the longest x2 1.22 us: diffuse(): scale_flux * flux_east]
    select_n x7 -> x0, other arithmetic: 4.61 us -> none  [the longest x4 4.24 us: limit_ratio(): jnp.where(supply > headroom, headroom / jnp.where(supply > headroom, supp...]
    unnamed x28 -> x14, local copies, waits for them, and re-layouts: 3.62 us -> 6.24 us
    slice x17 -> x0, local copies, waits for them, and re-layouts: 2.55 us -> none  [the longest x8 1.15 us: extreme_near(): above_vals = jnp.concatenate([center[:1], center[:-1]], 0)]
    concatenate x8 -> x0, other arithmetic: 1.91 us -> none  [the longest x4 1.35 us: extend_rim(): jnp.concatenate([tall_field[:, :tall_field.shape[1] - width, :], north_ro...]
  transfers between devices with their start and end apart: 27 -> 0, of which waited for: 14 -> 0; matrix products, arithmetic and copies ran while one was open for 2% -> 0% of each run, Pallas kernels for 0% -> 0%
where the time goes in v1:
time: 37.9 us; the launch traced here: 37.6 us
  Pallas kernels  30 us (79%)
  local copies, waits for them, and re-layouts  6.24 us (16%)
  between operations  1.3 us (3%)
    pallas_call x1, Pallas kernels, on_device(): pl.pallas_call(kernel, out_shape=(jax.ShapeDtypeStruct(t.shape, f32), jax...  30 us
    unnamed x14, local copies, waits for them, and re-layouts  6.24 us

profile of v1, /device:TPU:96, one launch (start us, length us, event | category | flops | bytes accessed | tf_op | source)
XLA Modules:
  0.0 37.6 jit_solution(12734049906860820175)
XLA Ops:
  1.3 0.0 copy-start
  1.3 0.9 %copy-done = f32[12,16,128]{2,1,0:T(8,128)S(1)} copy-done((f32[12,16,128]{2,1,0:T(8,128)S(1)}, f32[12,16,128]{2,1,0:T(8,128)}, u32[]{:S(2)}) %copy-start) | copy-done | bytes 98328
  2.2 0.0 copy-start.1
  2.2 0.9 %copy-done.1 = f32[12,16,128]{2,1,0:T(8,128)S(1)} copy-done((f32[12,16,128]{2,1,0:T(8,128)S(1)}, f32[12,16,128]{2,1,0:T(8,128)}, u32[]{:S(2)}) %copy-start.1) | copy-done | bytes 98328
  3.1 0.0 copy-start.2
  3.1 0.9 %copy-done.2 = f32[12,16,128]{2,1,0:T(8,128)S(1)} copy-done((f32[12,16,128]{2,1,0:T(8,128)S(1)}, f32[12,16,128]{2,1,0:T(8,128)}, u32[]{:S(2)}) %copy-start.2) | copy-done | bytes 98328
  4.0 0.0 copy-start.3
  4.0 0.9 %copy-done.3 = f32[12,16,128]{2,1,0:T(8,128)S(1)} copy-done((f32[12,16,128]{2,1,0:T(8,128)S(1)}, f32[12,16,128]{2,1,0:T(8,128)}, u32[]{:S(2)}) %copy-start.3) | copy-done | bytes 98328
  4.9 0.0 copy-start.4
  4.9 0.7 %copy-done.4 = s32[16,128]{1,0:T(8,128)S(1)} copy-done((s32[16,128]{1,0:T(8,128)S(1)}, s32[16,128]{1,0:T(8,128)}, u32[]{:S(2)}) %copy-start.4) | copy-done | bytes 8216
  5.5 0.0 copy-start.5
  5.5 0.7 %copy-done.5 = s32[16,128]{1,0:T(8,128)S(1)} copy-done((s32[16,128]{1,0:T(8,128)S(1)}, s32[16,128]{1,0:T(8,128)}, u32[]{:S(2)}) %copy-start.5) | copy-done | bytes 8216
  6.2 30.0 %shard_map.86 = (f32[12,16,128]{2,1,0:T(8,128)S(1)}, f32[12,16,128]{2,1,0:T(8,128)S(1)}) custom-call(f32[12,16,128]{2,1,0:T(8,128)S(1)} %copy-done, f32[12,16,128]{2,1,0:T(8,128)S(1)} %copy-done.1, f32[12,16,128]{2,1,0:T(8,128)S(1)} %copy-done.2, f32[12,16,128]{2,1,0:T(8,128)S(1)} %copy-done.3, s32[1,1]{1,0:T(1,128)S(6)} %copy.11.flag_ref, ...), custom_call_target="tpu_custom_call" | custom-call | tf_op jit(solution)/shard_map/pallas_call | solution.py:573
  36.3 0.6 %copy.12 = f32[12,16,128]{2,1,0:T(8,128)} copy(f32[12,16,128]{2,1,0:T(8,128)S(1)} %get-tuple-element.4) | data formatting | bytes 196608
  36.9 0.6 %copy.13 = f32[12,16,128]{2,1,0:T(8,128)} copy(f32[12,16,128]{2,1,0:T(8,128)S(1)} %get-tuple-element.5) | data formatting | bytes 196608
Async XLA Ops:
  1.3 0.9 %copy-start = (f32[12,16,128]{2,1,0:T(8,128)S(1)}, f32[12,16,128]{2,1,0:T(8,128)}, u32[]{:S(2)}) copy-start(f32[12,16,128]{2,1,0:T(8,128)} %t_hbm.1) | copy-start | bytes 294916
  2.2 0.9 %copy-start.1 = (f32[12,16,128]{2,1,0:T(8,128)S(1)}, f32[12,16,128]{2,1,0:T(8,128)}, u32[]{:S(2)}) copy-start(f32[12,16,128]{2,1,0:T(8,128)} %s_hbm.1) | copy-start | bytes 294916
  3.1 0.9 %copy-start.2 = (f32[12,16,128]{2,1,0:T(8,128)S(1)}, f32[12,16,128]{2,1,0:T(8,128)}, u32[]{:S(2)}) copy-start(f32[12,16,128]{2,1,0:T(8,128)} %u_hbm.1) | copy-start | bytes 294916
  4.0 0.9 %copy-start.3 = (f32[12,16,128]{2,1,0:T(8,128)S(1)}, f32[12,16,128]{2,1,0:T(8,128)}, u32[]{:S(2)}) copy-start(f32[12,16,128]{2,1,0:T(8,128)} %v_hbm.1) | copy-start | bytes 294916
  4.9 0.7 %copy-start.4 = (s32[16,128]{1,0:T(8,128)S(1)}, s32[16,128]{1,0:T(8,128)}, u32[]{:S(2)}) copy-start(s32[16,128]{1,0:T(8,128)} %point_ref.1) | copy-start | bytes 24580
  5.5 0.7 %copy-start.5 = (s32[16,128]{1,0:T(8,128)S(1)}, s32[16,128]{1,0:T(8,128)}, u32[]{:S(2)}) copy-start(s32[16,128]{1,0:T(8,128)} %count_ref.1) | copy-start | bytes 24580

commit v2 on v1

--- a/solution.py
+++ b/solution.py
@@ -80,7 +80,7 @@
         return tuple(out)
 
     zero = [jnp.zeros((n, 128), jnp.float32) for _, n, _, _ in wins]
-    lax.fori_loop(0, nk, body, tuple((x, tuple(x for _ in z["t"])) for x in zero))
+    lax.fori_loop(0, nk, body, tuple((x, tuple(x for _ in z["t"])) for x in zero), unroll=nk)
 
 
 def stage_ratio(z, wins):
@@ -117,7 +117,7 @@
             out.append(tuple(tops))
         return tuple(out)
 
-    lax.fori_loop(0, nk, body, tuple(tuple(jnp.zeros((n, 128), jnp.float32) for _ in z["t"]) for _, n, _, _ in wins))
+    lax.fori_loop(0, nk, body, tuple(tuple(jnp.zeros((n, 128), jnp.float32) for _ in z["t"]) for _, n, _, _ in wins), unroll=nk)
 
 
 def stage_limit(z, wins):
@@ -156,7 +156,7 @@
             out.append(tuple(tops))
         return tuple(out)
 
-    lax.fori_loop(0, nk, body, tuple(tuple(jnp.zeros((n, 128), jnp.float32) for _ in z["t"]) for _, n, _, _ in wins))
+    lax.fori_loop(0, nk, body, tuple(tuple(jnp.zeros((n, 128), jnp.float32) for _ in z["t"]) for _, n, _, _ in wins), unroll=nk)
 
 
 def clip_slope(x):
@@ -230,7 +230,7 @@
         x = jnp.zeros((n, 128), jnp.float32)
         xs = tuple(x for _ in range(nt))
         start.append((x, x, x, xs, xs, xs, xs, xs))
-    last = lax.fori_loop(0, nk, body, tuple(start))
+    last = lax.fori_loop(0, nk, body, tuple(start), unroll=nk // 2)
     for wi, ((f, *_), old) in enumerate(zip(stat, last)):
         for m in range(nt):
             emit(0, wi, m, jnp.where(0.0 < f, old[6][m] + DIFF_SCALE * old[7][m], 0.0))
@@ -241,10 +241,10 @@
 
 
 def kernel(
-    t_hbm, s_hbm, u_hbm, v_hbm, flag_ref, point_ref, count_ref,
-    t_out, s_out,
-    tr, u, v, floor, low, mx, mn, ax, ay, az, rin, rout, adv,
-    e_tr, e_u, e_v, e_floor, e_low, e_mx, e_mn, e_ax, e_ay, e_az, e_rin, e_rout, e_adv, e_res,
+    t_hbm, s_hbm, u_hbm, v_hbm, flag_hbm, point_hbm, count_hbm,
+    t_out, s_out, e_res,
+    flag_ref, point_ref, count_ref, tr, u, v, floor, low, mx, mn, ax, ay, az, rin, rout, adv,
+    e_tr, e_u, e_v, e_floor, e_low, e_mx, e_mn, e_ax, e_ay, e_az, e_rin, e_rout, e_adv,
     row_out, row_in, strip_out, fold_out, strip_in, corner_in,
     load_sem, send_sem, recv_sem,
 ):
@@ -299,11 +299,15 @@
         pltpu.make_async_copy(src, dst.at[:, 8:24, :], load_sem.at[i])
         for i, (src, dst) in enumerate(((t_hbm, tr.at[0]), (s_hbm, tr.at[1]), (u_hbm, u), (v_hbm, v)))
     ]
+    loads += [
+        pltpu.make_async_copy(src, dst, load_sem.at[4 + i])
+        for i, (src, dst) in enumerate(((flag_hbm, flag_ref), (point_hbm, point_ref), (count_hbm, count_ref)))
+    ]
     for copy in loads:
         copy.start()
-    floor[8:24, :] = (count_ref[...] * point_ref[...] * flag_ref[...]).astype(jnp.float32)
     for copy in loads:
         copy.wait()
+    floor[8:24, :] = (count_ref[...] * point_ref[...] * flag_ref[...]).astype(jnp.float32)
 
     fields = ((tr.at[0], tr.at[1]), (u, v))
     for g, (a, b) in enumerate(fields):
@@ -463,37 +467,18 @@
     @pl.when(at_south)
     def _():
         row_in[1] = jnp.zeros(row_in.shape[1:], jnp.float32)
-        corner_in[corner[SE]] = jnp.zeros(corner_in.shape[1:], jnp.float32)
-        corner_in[corner[SW]] = jnp.zeros(corner_in.shape[1:], jnp.float32)
 
     @pl.when(jnp.logical_not(at_south))
     def _():
-        for copy in north_sends:
-            copy.wait_recv()
-        for copy in south_sends:
-            copy.wait_send()
+        north_sends[0].wait_recv()
 
     @pl.when(jnp.logical_not(at_north))
     def _():
-        for copy in south_sends:
-            copy.wait_recv()
-        for copy in north_sends:
-            copy.wait_send()
+        south_sends[0].wait_recv()
 
     @pl.when(at_north)
     def _():
-        fold_sends[0].wait()
-        for copy, local, own in ((fold_sends[1], ne_local, ne_self), (fold_sends[2], nw_local, nw_self)):
-            @pl.when(own)
-            def _():
-                local.wait()
-
-            @pl.when(jnp.logical_not(own))
-            def _():
-                copy.wait()
-
-    for copy in side_sends:
-        copy.wait()
+        fold_sends[0].wait_recv()
 
     for slot, row in ((1, 4), (0, 24)):
         for g, (a, b) in enumerate(fields):
@@ -501,6 +486,52 @@
                 a[k, row : row + 4, :] = row_in[slot, g * nk + k, 0:4, :]
                 b[k, row : row + 4, :] = row_in[slot, g * nk + k, 4:8, :]
         floor[row : row + 4, :] = row_in[slot, 2 * nk, 0:4, :]
+
+    stage_flux(main, [(4, 8, 1, 5), (20, 8, 3, 7)])
+    stage_ratio(main, [(4, 8, 2, 6), (20, 8, 2, 6)])
+    stage_limit(main, [(4, 8, 3, 7), (20, 8, 1, 5)])
+
+    def emit_outer(k, wi, m, val):
+        if wi == 0:
+            outs[m][k, 0:4, :] = val[4:8]
+        else:
+            outs[m][k, 12:16, :] = val[4:8]
+
+    stage_diffuse(main, [(4, 8, 4, 8), (16, 8, 4, 8)], emit_outer)
+
+    @pl.when(at_south)
+    def _():
+        corner_in[corner[SE]] = jnp.zeros(corner_in.shape[1:], jnp.float32)
+        corner_in[corner[SW]] = jnp.zeros(corner_in.shape[1:], jnp.float32)
+
+    @pl.when(jnp.logical_not(at_south))
+    def _():
+        for copy in north_sends[1:]:
+            copy.wait_recv()
+        for copy in south_sends:
+            copy.wait_send()
+
+    @pl.when(jnp.logical_not(at_north))
+    def _():
+        for copy in south_sends[1:]:
+            copy.wait_recv()
+        for copy in north_sends:
+            copy.wait_send()
+
+    @pl.when(at_north)
+    def _():
+        fold_sends[0].wait_send()
+        for copy, local, own in ((fold_sends[1], ne_local, ne_self), (fold_sends[2], nw_local, nw_self)):
+            @pl.when(own)
+            def _():
+                local.wait()
+
+            @pl.when(jnp.logical_not(own))
+            def _():
+                copy.wait()
+
+    for copy in side_sends:
+        copy.wait()
 
     strip_tile(0)
     strip_tile(24)
@@ -523,18 +554,6 @@
                 e_u[level, rows, :] = jnp.where(halo, pltpu.roll(y, 120, 1), e_u[level, rows, :])
                 e_v[level, rows, :] = jnp.where(halo, pltpu.roll(y, 112, 1), e_v[level, rows, :])
 
-    stage_flux(main, [(4, 8, 1, 5), (20, 8, 3, 7)])
-    stage_ratio(main, [(4, 8, 2, 6), (20, 8, 2, 6)])
-    stage_limit(main, [(4, 8, 3, 7), (20, 8, 1, 5)])
-
-    def emit_outer(k, wi, m, val):
-        if wi == 0:
-            outs[m][k, 0:4, :] = val[4:8]
-        else:
-            outs[m][k, 12:16, :] = val[4:8]
-
-    stage_diffuse(main, [(4, 8, 4, 8), (16, 8, 4, 8)], emit_outer)
-
     def strip_density(one):
         x = one[0]
         low_half = lane_iota(x.shape[0]) < 64
@@ -554,12 +573,19 @@
 
     stage_diffuse(strips, [(4, 24, 4, 20)], emit_strip)
 
+
+def finish(t_ref, s_ref, e_res, t_hbm, s_hbm, t_buf, s_buf, sem):
     lane16 = lane_iota(16)
     rim = jnp.logical_or(lane16 < 4, lane16 >= 124)
-    for m in range(2):
+    copies = []
+    for m, (ref, buf, out) in enumerate(((t_ref, t_buf, t_hbm), (s_ref, s_buf, s_hbm))):
         back = jnp.where(lane16 < 4, lane16 + 20, jnp.where(lane16 >= 124, lane16 - 116, 0)) + 64 * m
-        for k in range(nk):
-            outs[m][k] = jnp.where(rim, jnp.take_along_axis(e_res[k], back, axis=1), outs[m][k])
+        for k in range(ref.shape[0]):
+            buf[k] = jnp.where(rim, jnp.take_along_axis(e_res[k], back, axis=1), ref[k])
+        copies.append(pltpu.make_async_copy(buf, out, sem.at[m]))
+        copies[-1].start()
+    for copy in copies:
+        copy.wait()
 
 
 def on_device(t, s, u, v, flag, point, count):
@@ -569,27 +595,37 @@
     big = lambda: vm(2, nk, 32, 128)
     one = lambda: vm(nk, 32, 128)
     whole = pl.BlockSpec(memory_space=pltpu.VMEM)
-    hbm = pl.BlockSpec(memory_space=pl.ANY)
-    return pl.pallas_call(
+    hbm = pl.BlockSpec(memory_space=pltpu.HBM)
+    part = pltpu.VMEM(t.shape, f32)
+    main_t, main_s, strips = pl.pallas_call(
         kernel,
-        out_shape=(jax.ShapeDtypeStruct(t.shape, f32), jax.ShapeDtypeStruct(s.shape, f32)),
-        in_specs=[hbm] * 4 + [whole] * 3,
-        out_specs=(whole, whole),
+        out_shape=(part, part, part),
+        in_specs=[hbm] * 7,
+        out_specs=(whole, whole, whole),
         scratch_shapes=[
+            pltpu.VMEM(flag.shape, flag.dtype), pltpu.VMEM(point.shape, point.dtype), pltpu.VMEM(count.shape, count.dtype),
             big(), one(), one(), vm(32, 128),
             *[big() for _ in range(9)],
             one(), one(), one(), vm(32, 128),
             *[one() for _ in range(9)],
-            vm(nk, 16, 128),
             vm(2, 2 * nk + 1, 8, 128), vm(2, 2 * nk + 1, 8, 128),
             vm(nk // 2 + 1, 16, 128), vm(nk // 2 + 1, 8, 128),
             vm(2, nk // 2 + 1, 16, 128), vm(4, nk // 2 + 1, 8, 128),
-            pltpu.SemaphoreType.DMA((4,)), pltpu.SemaphoreType.DMA((8,)), pltpu.SemaphoreType.DMA((8,)),
+            pltpu.SemaphoreType.DMA((7,)), pltpu.SemaphoreType.DMA((8,)), pltpu.SemaphoreType.DMA((8,)),
         ],
         compiler_params=pltpu.CompilerParams(
-            collective_id=0, has_side_effects=True, vmem_limit_bytes=32 * 1024 * 1024
+            collective_id=0, has_side_effects=True, vmem_limit_bytes=60 * 1024 * 1024
         ),
     )(t, s, u, v, flag, point, count)
+    result = jax.ShapeDtypeStruct(t.shape, f32)
+    return pl.pallas_call(
+        finish,
+        out_shape=(result, result),
+        in_specs=[whole] * 3,
+        out_specs=(hbm, hbm),
+        scratch_shapes=[vm(*t.shape), vm(*t.shape), pltpu.SemaphoreType.DMA((2,))],
+        compiler_params=pltpu.CompilerParams(vmem_limit_bytes=4 * 1024 * 1024),
+    )(main_t, main_s, strips)
 
 
 def solution(mesh):

time: 37.9 us -> 22.7 us (0.60)
  the two profiles are of different devices: /device:TPU:96 before, /device:TPU:64 now
where the time goes in v2:
time: 22.7 us; the launch traced here: 22.5 us
  Pallas kernels  21.2 us (93%)
  between operations  1.29 us (6%)
    pallas_call x1, Pallas kernels, on_device(): pl.pallas_call(kernel, out_shape=(part, part, part), in_specs=[hbm] * 7,...  20.5 us
    pallas_call x1, Pallas kernels, on_device(): pl.pallas_call(finish, out_shape=(result, result), in_specs=[whole] * 3,...  0.79 us

profile of v2, /device:TPU:64, one launch (start us, length us, event | category | flops | bytes accessed | tf_op | source)
XLA Modules:
  0.0 22.5 jit_solution(15123997151148939677)
XLA Ops:
  1.3 20.5 %shard_map.86 = (f32[12,16,128]{2,1,0:T(8,128)S(1)}, f32[12,16,128]{2,1,0:T(8,128)S(1)}, f32[12,16,128]{2,1,0:T(8,128)S(1)}) custom-call(f32[12,16,128]{2,1,0:T(8,128)} %t_hbm.1, f32[12,16,128]{2,1,0:T(8,128)} %s_hbm.1, f32[12,16,128]{2,1,0:T(8,128)} %u_hbm.1, f32[12,16,128]{2,1,0:T(8,128)} %v_hbm.1, s32[1,1]{1,0:T(1,128)S(6)} %copy.9.flag_hbm, ...), custom_call_target="tpu_custom_call" | custom-call | tf_op jit(solution)/shard_map/pallas_call | solution.py:600
  21.7 0.8 %shard_map.87 = (f32[12,16,128]{2,1,0:T(8,128)}, f32[12,16,128]{2,1,0:T(8,128)}) custom-call(f32[12,16,128]{2,1,0:T(8,128)S(1)} %get-tuple-element.5.t_ref, f32[12,16,128]{2,1,0:T(8,128)S(1)} %get-tuple-element.6.s_ref, f32[12,16,128]{2,1,0:T(8,128)S(1)} %get-tuple-element.7.e_res), custom_call_target="tpu_custom_call" | custom-call | tf_op jit(solution)/shard_map/pallas_call | solution.py:621

commit v3 on v2

--- a/solution.py
+++ b/solution.py
@@ -33,6 +33,58 @@
 
 def south_of(x):
     return pltpu.roll(x, 1, 0)
+
+
+def lane_iota(rows):
+    return lax.broadcasted_iota(jnp.int32, (rows, 128), 1)
+
+
+def upper_lanes(rows):
+    return lax.rem(lane_iota(rows), 64) < 32
+
+
+def to_upper(x):
+    return jnp.where(upper_lanes(x.shape[0]), pltpu.roll(x, 96, 1), 0.0)
+
+
+def to_lower(x):
+    return jnp.where(upper_lanes(x.shape[0]), 0.0, pltpu.roll(x, 32, 1))
+
+
+def above(z, ref, k, r0, n):
+    if not z["split"]:
+        return ref[jnp.maximum(k - 1, 0), r0 : r0 + n, :]
+    if k > 0:
+        return ref[k - 1, r0 : r0 + n, :]
+    last = z["u"].shape[0] - 1
+    return jnp.where(upper_lanes(n), ref[0, r0 : r0 + n, :], pltpu.roll(ref[last, r0 : r0 + n, :], 32, 1))
+
+
+def below(z, ref, k, r0, n):
+    last = z["u"].shape[0] - 1
+    if not z["split"]:
+        return ref[jnp.minimum(k + 1, last), r0 : r0 + n, :]
+    if k < last:
+        return ref[k + 1, r0 : r0 + n, :]
+    return jnp.where(upper_lanes(n), pltpu.roll(ref[0, r0 : r0 + n, :], 96, 1), ref[last, r0 : r0 + n, :])
+
+
+def upward(z, body, carry, unroll):
+    nk = z["u"].shape[0]
+    if z["split"]:
+        for k in range(nk - 1, -1, -1):
+            carry = body(k, jnp.float32(k), carry)
+        return carry
+
+    def step(i, carry):
+        k = nk - 1 - i
+        return body(k, k.astype(jnp.float32), carry)
+
+    return lax.fori_loop(0, nk, step, carry, unroll=unroll)
+
+
+def nothing(z, wins):
+    return tuple(tuple(jnp.zeros((n, 128), jnp.float32) for _ in z["t"]) for _, n, _, _ in wins)
 
 
 def stage_flux(z, wins):
@@ -44,17 +96,18 @@
         f_n = jnp.minimum(f, z["f"][r0 + 1 : r0 + 1 + n, :])
         stat.append((f, f_e, f_n))
 
-    def body(i, carry):
-        k = nk - 1 - i
-        kk = k.astype(jnp.float32)
-        up_k = jnp.maximum(k - 1, 0)
+    def velocities(k, kk, r0, n, f_e, f_n):
+        u = z["u"][k, r0 : r0 + n, :]
+        u_e = jnp.where(kk < f_e, FACE_SCALE * (u + east_of(u)), 0.0)
+        v = z["v"][k, r0 : r0 + n, :]
+        v_n = jnp.where(kk < f_n, FACE_SCALE * (v + z["v"][k, r0 + 1 : r0 + 1 + n, :]), 0.0)
+        return u_e, v_n, u_e - west_of(u_e) + v_n - south_of(v_n)
+
+    def body(k, kk, carry):
         out = []
         for (r0, n, lo, hi), (f, f_e, f_n), (w_old, bottoms) in zip(wins, stat, carry):
-            u = z["u"][k, r0 : r0 + n, :]
-            u_e = jnp.where(kk < f_e, FACE_SCALE * (u + east_of(u)), 0.0)
-            v = z["v"][k, r0 : r0 + n, :]
-            v_n = jnp.where(kk < f_n, FACE_SCALE * (v + z["v"][k, r0 + 1 : r0 + 1 + n, :]), 0.0)
-            w = w_old - (u_e - west_of(u_e) + v_n - south_of(v_n))
+            u_e, v_n, gain = velocities(k, kk, r0, n, f_e, f_n)
+            w = w_old - gain
             abs_u, abs_v, abs_w = jnp.abs(u_e), jnp.abs(v_n), jnp.abs(w)
             wet = kk < f
             tops = []
@@ -62,7 +115,7 @@
                 c = t[k, r0 : r0 + n, :]
                 e = east_of(c)
                 nn = t[k, r0 + 1 : r0 + 1 + n, :]
-                up = t[up_k, r0 : r0 + n, :]
+                up = above(z, t, k, r0, n)
                 a_e = abs_u * (e - c)
                 l_e = u_e * (c + e) - a_e
                 a_n = abs_v * (nn - c)
@@ -79,16 +132,26 @@
             out.append((w, tuple(tops)))
         return tuple(out)
 
-    zero = [jnp.zeros((n, 128), jnp.float32) for _, n, _, _ in wins]
-    lax.fori_loop(0, nk, body, tuple((x, tuple(x for _ in z["t"])) for x in zero), unroll=nk)
+    start = []
+    for (r0, n, _, _), (f, f_e, f_n) in zip(wins, stat):
+        w = jnp.zeros((n, 128), jnp.float32)
+        flows = tuple(w for _ in z["t"])
+        if z["split"]:
+            for k in range(nk):
+                w = w - velocities(k, jnp.float32(k), r0, n, f_e, f_n)[2]
+            w = to_upper(w)
+            flows = []
+            for t in z["t"]:
+                up, c = t[nk - 1, r0 : r0 + n, :], below(z, t, nk - 1, r0, n)
+                flows.append(w * (c + up) - jnp.abs(w) * (up - c))
+        start.append((w, tuple(flows)))
+    upward(z, body, tuple(start), nk)
 
 
 def stage_ratio(z, wins):
     nk = z["u"].shape[0]
 
-    def body(i, carry):
-        k = nk - 1 - i
-        up_k, down_k = jnp.maximum(k - 1, 0), jnp.minimum(k + 1, nk - 1)
+    def body(k, kk, carry):
         out = []
         for (r0, n, lo, hi), bottoms in zip(wins, carry):
             tops = []
@@ -96,7 +159,7 @@
                 def near(ref, pick):
                     c = ref[k, r0 : r0 + n, :]
                     horizontal = pick(pick(east_of(c), west_of(c)), pick(ref[k, r0 + 1 : r0 + 1 + n, :], ref[k, r0 - 1 : r0 - 1 + n, :]))
-                    return pick(pick(c, horizontal), pick(ref[up_k, r0 : r0 + n, :], ref[down_k, r0 : r0 + n, :]))
+                    return pick(pick(c, horizontal), pick(above(z, ref, k, r0, n), below(z, ref, k, r0, n)))
 
                 big, small = near(z["mx"][m], jnp.maximum), near(z["mn"][m], jnp.minimum)
                 low = z["low"][m][k, r0 : r0 + n, :]
@@ -117,37 +180,37 @@
             out.append(tuple(tops))
         return tuple(out)
 
-    lax.fori_loop(0, nk, body, tuple(tuple(jnp.zeros((n, 128), jnp.float32) for _ in z["t"]) for _, n, _, _ in wins), unroll=nk)
+    start = nothing(z, wins)
+    if z["split"]:
+        start = tuple(tuple(to_upper(a[0, r0 : r0 + n, :]) for a in z["az"]) for r0, n, _, _ in wins)
+    upward(z, body, start, nk)
+
+
+def limited(anti, r_in, r_out, far_in, far_out):
+    return anti * jnp.where(anti >= 0, jnp.minimum(far_in, r_out), jnp.minimum(r_in, far_out))
 
 
 def stage_limit(z, wins):
     nk = z["u"].shape[0]
     stat = [z["f"][r0 : r0 + n, :] for r0, n, _, _ in wins]
 
-    def body(i, carry):
-        k = nk - 1 - i
-        kk = k.astype(jnp.float32)
-        up_k = jnp.maximum(k - 1, 0)
+    def rise(m, k, r0, n):
+        r_in, r_out = z["rin"][m][k, r0 : r0 + n, :], z["rout"][m][k, r0 : r0 + n, :]
+        far_in, far_out = above(z, z["rin"][m], k, r0, n), above(z, z["rout"][m], k, r0, n)
+        return limited(z["az"][m][k, r0 : r0 + n, :], r_in, r_out, far_in, far_out)
+
+    def body(k, kk, carry):
         out = []
         for (r0, n, lo, hi), f, bottoms in zip(wins, stat, carry):
             tops = []
             for m in range(len(z["t"])):
                 r_in, r_out = z["rin"][m][k, r0 : r0 + n, :], z["rout"][m][k, r0 : r0 + n, :]
-
-                def limited(anti, far_in, far_out):
-                    return anti * jnp.where(anti >= 0, jnp.minimum(far_in, r_out), jnp.minimum(r_in, far_out))
-
-                f_e = limited(z["ax"][m][k, r0 : r0 + n, :], east_of(r_in), east_of(r_out))
+                f_e = limited(z["ax"][m][k, r0 : r0 + n, :], r_in, r_out, east_of(r_in), east_of(r_out))
                 f_n = limited(
-                    z["ay"][m][k, r0 : r0 + n, :],
-                    z["rin"][m][k, r0 + 1 : r0 + 1 + n, :],
-                    z["rout"][m][k, r0 + 1 : r0 + 1 + n, :],
+                    z["ay"][m][k, r0 : r0 + n, :], r_in, r_out,
+                    z["rin"][m][k, r0 + 1 : r0 + 1 + n, :], z["rout"][m][k, r0 + 1 : r0 + 1 + n, :],
                 )
-                f_t = limited(
-                    z["az"][m][k, r0 : r0 + n, :],
-                    z["rin"][m][up_k, r0 : r0 + n, :],
-                    z["rout"][m][up_k, r0 : r0 + n, :],
-                )
+                f_t = rise(m, k, r0, n)
                 low = z["low"][m][k, r0 : r0 + n, :]
                 new = low - ((f_e - west_of(f_e)) + (f_n - south_of(f_n)) + (f_t - bottoms[m]))
                 new = jnp.where(kk < f, new, 0.0)
@@ -156,7 +219,10 @@
             out.append(tuple(tops))
         return tuple(out)
 
-    lax.fori_loop(0, nk, body, tuple(tuple(jnp.zeros((n, 128), jnp.float32) for _ in z["t"]) for _, n, _, _ in wins), unroll=nk)
+    start = nothing(z, wins)
+    if z["split"]:
+        start = tuple(tuple(to_upper(rise(m, 0, r0, n)) for m in range(len(z["t"]))) for r0, n, _, _ in wins)
+    upward(z, body, start, nk)
 
 
 def clip_slope(x):
@@ -176,31 +242,34 @@
     def inverse(grads):
         return pl.reciprocal(jnp.maximum(-dens(grads), strat_floor))
 
-    def body(i, carry):
-        k = nk - 1 - i
-        kk = k.astype(jnp.float32)
-        up_k = jnp.maximum(k - 1, 0)
-        below_k = jnp.minimum(k + 1, nk - 1)
-        not_top = (k >= 1).astype(jnp.float32)
+    def vertical(k, kk, r0, n, f, far_n):
+        gz = [jnp.where(kk < f, above(z, a, k, r0, n) - a[k, r0 : r0 + n, :], 0.0) for a in z["adv"]]
+        gz_n = [jnp.where(kk < far_n, above(z, a, k, r0 + 1, n) - a[k, r0 + 1 : r0 + 1 + n, :], 0.0) for a in z["adv"]]
+        inv = inverse(gz)
+        return inv, east_of(inv), inverse(gz_n), tuple(gz), tuple(east_of(g) for g in gz), tuple(gz_n)
+
+    def body(k, kk, carry):
         out = []
         for wi, ((r0, n, _, _), (f, far_e, far_n, f_e, f_n), old) in enumerate(zip(wins, stat, carry)):
+            if not z["split"]:
+                not_top = (k >= 1).astype(jnp.float32)
+            elif k == 0:
+                not_top = jnp.where(upper_lanes(n), 0.0, 1.0)
             here = [a[k, r0 : r0 + n, :] for a in z["adv"]]
             north = [a[k, r0 + 1 : r0 + 1 + n, :] for a in z["adv"]]
-            gz = [jnp.where(kk < f, a[up_k, r0 : r0 + n, :] - c, 0.0) for a, c in zip(z["adv"], here)]
-            gz_n = [jnp.where(kk < far_n, a[up_k, r0 + 1 : r0 + 1 + n, :] - c, 0.0) for a, c in zip(z["adv"], north)]
-            gz_e = [east_of(g) for g in gz]
-            inv, inv_n = inverse(gz), inverse(gz_n)
-            inv_e = east_of(inv)
+            inv, inv_e, inv_n, gz, gz_e, gz_n = vertical(k, kk, r0, n, f, far_n)
             gx = [jnp.where(kk < f_e, east_of(c) - c, 0.0) for c in here]
             gy = [jnp.where(kk < f_n, b - c, 0.0) for b, c in zip(north, here)]
             rx, ry = dens(gx), dens(gy)
-            (o_inv, o_inv_e, o_inv_n, o_gz, o_gz_e, o_gz_n, o_part, o_top) = old
+            (o_inv, o_inv_e, o_inv_n, o_gz, o_gz_e, o_gz_n), o_part, o_top = old
             low_here, low_e, low_n = kk + 1.0 < f, kk + 1.0 < far_e, kk + 1.0 < far_n
             s_x = [clip_slope(rx * q) for q in (inv, inv_e, o_inv, o_inv_e)]
             s_y = [clip_slope(ry * q) for q in (inv, inv_n, o_inv, o_inv_n)]
             parts, tops = [], []
             for m in range(nt):
-                gx_top, gy_top = gx[m] * not_top, gy[m] * not_top
+                gx_top, gy_top = gx[m], gy[m]
+                if not z["split"] or k == 0:
+                    gx_top, gy_top = gx_top * not_top, gy_top * not_top
                 hx = (
                     gx_top + s_x[0] * gz[m],
                     gx_top + s_x[1] * gz_e[m],
@@ -218,26 +287,34 @@
                 top = (s_x[0] * hx[0] + west_of(s_x[1] * hx[1])) + (s_y[0] * hy[0] + south_of(s_y[1] * hy[1]))
                 bottom = (s_x[2] * hx[2] + west_of(s_x[3] * hx[3])) + (s_y[2] * hy[2] + south_of(s_y[3] * hy[3]))
                 rise = o_top[m] + bottom
-                done = jnp.where(kk + 1.0 < f, o_part[m] + DIFF_SCALE * rise, 0.0)
-                emit(below_k, wi, m, done)
+                if z["split"] and k == nk - 1:
+                    bottom_lower[wi, m] = to_lower(bottom)
+                else:
+                    done = jnp.where(kk + 1.0 < f, o_part[m] + DIFF_SCALE * rise, 0.0)
+                    emit(k + 1 if z["split"] else jnp.minimum(k + 1, nk - 1), wi, m, done)
                 parts.append(here[m] + DIFF_SCALE * ((flux_e - west_of(flux_e)) + (flux_n - south_of(flux_n)) - rise))
                 tops.append(top)
-            out.append((inv, inv_e, inv_n, tuple(gz), tuple(gz_e), tuple(gz_n), tuple(parts), tuple(tops)))
+            out.append(((inv, inv_e, inv_n, gz, gz_e, gz_n), tuple(parts), tuple(tops)))
         return tuple(out)
 
+    bottom_lower = {}
     start = []
-    for _, n, _, _ in wins:
+    for (r0, n, _, _), (f, _, far_n, *_) in zip(wins, stat):
         x = jnp.zeros((n, 128), jnp.float32)
         xs = tuple(x for _ in range(nt))
-        start.append((x, x, x, xs, xs, xs, xs, xs))
-    last = lax.fori_loop(0, nk, body, tuple(start), unroll=nk // 2)
-    for wi, ((f, *_), old) in enumerate(zip(stat, last)):
+        first = (x, x, x, xs, xs, xs)
+        if z["split"]:
+            first = jax.tree.map(to_upper, vertical(0, jnp.float32(0), r0, n, f, far_n))
+        start.append((first, xs, xs))
+    last = upward(z, body, tuple(start), nk // 2)
+    for wi, ((r0, n, _, _), (f, *_), (_, parts, tops)) in enumerate(zip(wins, stat, last)):
         for m in range(nt):
-            emit(0, wi, m, jnp.where(0.0 < f, old[6][m] + DIFF_SCALE * old[7][m], 0.0))
-
-
-def lane_iota(rows):
-    return lax.broadcasted_iota(jnp.int32, (rows, 128), 1)
+            top = tops[m]
+            if z["split"]:
+                top = top + bottom_lower[wi, m]
+                late = jnp.where(nk - 1.0 < f, -DIFF_SCALE * to_upper(tops[m]), 0.0)
+                emit(nk - 1, wi, m, late, True)
+            emit(0, wi, m, jnp.where(0.0 < f, parts[m] + DIFF_SCALE * top, 0.0))
 
 
 def kernel(
@@ -339,37 +416,36 @@
                 row_out[0, g * nk + k, 4:8, :] = sign * turned(b[k, 16:24, :])[0:4]
         row_out[0, 2 * nk, 0:4, :] = turned(floor[16:24, :])[0:4]
 
-    p = lax.rem(lane8, 64)
+    p = lax.rem(lane8, 32)
     shift = jnp.where(p < 12, 116, jnp.where(p < 16, -12, jnp.where(p < 20, 108, -20)))
     strip_idx = lax.rem(p + shift + 128, 128)
-    first = lane8 < 64
+    first, upper = lane8 < 64, upper_lanes(8)
 
     def strip_tile(row):
+        rows = slice(row, row + 8)
+
         def gather(x):
             return jnp.take_along_axis(x, strip_idx, axis=1)
 
-        rows = slice(row, row + 8)
-        for k in range(nk):
-            e_tr[k, rows, :] = jnp.where(first, gather(tr[0, k, rows, :]), gather(tr[1, k, rows, :]))
-            e_u[k, rows, :] = gather(u[k, rows, :])
-            e_v[k, rows, :] = gather(v[k, rows, :])
-        e_floor[rows, :] = gather(floor[rows, :])
-
-    q = lax.rem(lane8, 32)
-    q_t = jnp.logical_and(q >= 12, q < 20)
-    q_u = jnp.logical_and(q >= 20, q < 28)
-    p32 = lax.rem(lane8 + 124, 64) < 32
+        def halves(ref, k):
+            return jnp.where(upper, gather(ref[k, rows, :]), gather(ref[k + half, rows, :]))
+
+        for k in range(half):
+            e_tr[k, rows, :] = jnp.where(first, halves(tr.at[0], k), halves(tr.at[1], k))
+            e_u[k, rows, :] = halves(u, k)
+            e_v[k, rows, :] = halves(v, k)
+        e_floor[rows, :] = gather(floor[rows, :]) - jnp.where(upper, 0.0, float(half))
+
+    q_t = jnp.logical_and(p >= 12, p < 20)
+    q_u = jnp.logical_and(p >= 20, p < 28)
     for row in (8, 16):
         strip_tile(row)
         rows = slice(row, row + 8)
         for k in range(half):
-            def packed(level):
-                return jnp.where(
-                    q_t, e_tr[level, rows, :],
-                    jnp.where(q_u, pltpu.roll(e_u[level, rows, :], 8, 1), pltpu.roll(e_v[level, rows, :], 16, 1)),
-                )
-
-            strip_out[k, row - 8 : row, :] = jnp.where(p32, packed(k), pltpu.roll(packed(k + half), 32, 1))
+            strip_out[k, row - 8 : row, :] = jnp.where(
+                q_t, e_tr[k, rows, :],
+                jnp.where(q_u, pltpu.roll(e_u[k, rows, :], 8, 1), pltpu.roll(e_v[k, rows, :], 16, 1)),
+            )
         strip_out[half, row - 8 : row, :] = e_floor[rows, :]
 
     @pl.when(at_north)
@@ -447,7 +523,7 @@
         copy.start()
 
     main = dict(
-        t=[tr.at[0], tr.at[1]], u=u, v=v, f=floor,
+        split=False, t=[tr.at[0], tr.at[1]], u=u, v=v, f=floor,
         density=lambda pair: haline_coef * pair[1] - thermal_coef * pair[0],
     )
     names = dict(low=low, mx=mx, mn=mn, ax=ax, ay=ay, az=az, rin=rin, rout=rout, adv=adv)
@@ -535,7 +611,6 @@
 
     strip_tile(0)
     strip_tile(24)
-    halo = jnp.logical_and(p >= 12, p < 20)
     from_east = lax.rem(lane8, 8) >= 4
     for row, east_ref, west_ref, at in (
         (0, corner_in.at[corner[SE]], corner_in.at[corner[SW]], 0),
@@ -547,12 +622,11 @@
         for k in range(half + 1):
             x = jnp.where(from_east, east_ref[k, at : at + 8, :], west_ref[k, at : at + 8, :])
             if k == half:
-                e_floor[rows, :] = jnp.where(halo, x, e_floor[rows, :])
+                e_floor[rows, :] = jnp.where(q_t, x, e_floor[rows, :])
                 continue
-            for level, y in ((k, x), (k + half, pltpu.roll(x, 96, 1))):
-                e_tr[level, rows, :] = jnp.where(halo, y, e_tr[level, rows, :])
-                e_u[level, rows, :] = jnp.where(halo, pltpu.roll(y, 120, 1), e_u[level, rows, :])
-                e_v[level, rows, :] = jnp.where(halo, pltpu.roll(y, 112, 1), e_v[level, rows, :])
+            e_tr[k, rows, :] = jnp.where(q_t, x, e_tr[k, rows, :])
+            e_u[k, rows, :] = jnp.where(q_t, pltpu.roll(x, 120, 1), e_u[k, rows, :])
+            e_v[k, rows, :] = jnp.where(q_t, pltpu.roll(x, 112, 1), e_v[k, rows, :])
 
     def strip_density(one):
         x = one[0]
@@ -561,15 +635,15 @@
         other = jnp.where(low_half, haline_coef, -thermal_coef)
         return own * x + other * pltpu.roll(x, 64, 1)
 
-    strips = dict(t=[e_tr], u=e_u, v=e_v, f=e_floor, density=strip_density)
+    strips = dict(split=True, t=[e_tr], u=e_u, v=e_v, f=e_floor, density=strip_density)
     names = dict(low=e_low, mx=e_mx, mn=e_mn, ax=e_ax, ay=e_ay, az=e_az, rin=e_rin, rout=e_rout, adv=e_adv)
     strips.update({name: [ref] for name, ref in names.items()})
     stage_flux(strips, [(4, 24, 0, 24)])
     stage_ratio(strips, [(4, 24, 0, 24)])
     stage_limit(strips, [(4, 24, 0, 24)])
 
-    def emit_strip(k, wi, m, val):
-        e_res[k] = val[4:20]
+    def emit_strip(k, wi, m, val, add=False):
+        e_res[k] = e_res[k] + val[4:20] if add else val[4:20]
 
     stage_diffuse(strips, [(4, 24, 4, 20)], emit_strip)
 
@@ -580,8 +654,10 @@
     copies = []
     for m, (ref, buf, out) in enumerate(((t_ref, t_buf, t_hbm), (s_ref, s_buf, s_hbm))):
         back = jnp.where(lane16 < 4, lane16 + 20, jnp.where(lane16 >= 124, lane16 - 116, 0)) + 64 * m
+        half = e_res.shape[0]
         for k in range(ref.shape[0]):
-            buf[k] = jnp.where(rim, jnp.take_along_axis(e_res[k], back, axis=1), ref[k])
+            edge = jnp.take_along_axis(e_res[k % half], back + 32 * (k // half), axis=1)
+            buf[k] = jnp.where(rim, edge, ref[k])
         copies.append(pltpu.make_async_copy(buf, out, sem.at[m]))
         copies[-1].start()
     for copy in copies:
@@ -599,15 +675,15 @@
     part = pltpu.VMEM(t.shape, f32)
     main_t, main_s, strips = pl.pallas_call(
         kernel,
-        out_shape=(part, part, part),
+        out_shape=(part, part, pltpu.VMEM((nk // 2, *t.shape[1:]), f32)),
         in_specs=[hbm] * 7,
         out_specs=(whole, whole, whole),
         scratch_shapes=[
             pltpu.VMEM(flag.shape, flag.dtype), pltpu.VMEM(point.shape, point.dtype), pltpu.VMEM(count.shape, count.dtype),
             big(), one(), one(), vm(32, 128),
             *[big() for _ in range(9)],
-            one(), one(), one(), vm(32, 128),
-            *[one() for _ in range(9)],
+            *[vm(nk // 2, 32, 128) for _ in range(3)], vm(32, 128),
+            *[vm(nk // 2, 32, 128) for _ in range(9)],
             vm(2, 2 * nk + 1, 8, 128), vm(2, 2 * nk + 1, 8, 128),
             vm(nk // 2 + 1, 16, 128), vm(nk // 2 + 1, 8, 128),
             vm(2, nk // 2 + 1, 16, 128), vm(4, nk // 2 + 1, 8, 128),

time: 22.7 us -> 19.9 us (0.88)
  Pallas kernels: 21.2 us -> 18.5 us
    pallas_call x1, Pallas kernels: 20.5 us -> 17.7 us  [on_device(): pl.pallas_call(kernel, out_shape=(part, part, pltpu.VMEM((nk // 2, *t.sha...]
where the time goes in v3:
time: 19.9 us; the launch traced here: 19.8 us
  Pallas kernels  18.5 us (93%)
  between operations  1.29 us (6%)
    pallas_call x1, Pallas kernels, on_device(): pl.pallas_call(kernel, out_shape=(part, part, pltpu.VMEM((nk // 2, *t.sha...  17.7 us
    pallas_call x1, Pallas kernels, on_device(): pl.pallas_call(finish, out_shape=(result, result), in_specs=[whole] * 3,...  0.79 us

profile of v3, /device:TPU:64, one launch (start us, length us, event | category | flops | bytes accessed | tf_op | source)
XLA Modules:
  0.0 19.8 jit_solution(6359908888527367230)
XLA Ops:
  1.3 17.7 %shard_map.86 = (f32[12,16,128]{2,1,0:T(8,128)S(1)}, f32[12,16,128]{2,1,0:T(8,128)S(1)}, f32[6,16,128]{2,1,0:T(8,128)S(1)}) custom-call(f32[12,16,128]{2,1,0:T(8,128)} %t_hbm.1, f32[12,16,128]{2,1,0:T(8,128)} %s_hbm.1, f32[12,16,128]{2,1,0:T(8,128)} %u_hbm.1, f32[12,16,128]{2,1,0:T(8,128)} %v_hbm.1, s32[1,1]{1,0:T(1,128)S(6)} %copy.9.flag_hbm, ...), custom_call_target="tpu_custom_call" | custom-call | tf_op jit(solution)/shard_map/pallas_call | solution.py:676
  19.0 0.8 %shard_map.87 = (f32[12,16,128]{2,1,0:T(8,128)}, f32[12,16,128]{2,1,0:T(8,128)}) custom-call(f32[12,16,128]{2,1,0:T(8,128)S(1)} %get-tuple-element.5.t_ref, f32[12,16,128]{2,1,0:T(8,128)S(1)} %get-tuple-element.6.s_ref, f32[6,16,128]{2,1,0:T(8,128)S(1)} %get-tuple-element.7.e_res), custom_call_target="tpu_custom_call" | custom-call | tf_op jit(solution)/shard_map/pallas_call | solution.py:697

commit v4 on v3

--- a/solution.py
+++ b/solution.py
@@ -20,7 +20,7 @@
 FACE_SCALE = 0.25 * time_step
 DIFF_SCALE = 0.25 * time_step * diffusivity
 
-EAST, WEST, NORTH, SOUTH, NE, NW, SE, SW = range(8)
+EAST, WEST, NORTH, SOUTH, CORNER_NORTH, CORNER_SOUTH = range(6)
 
 
 def east_of(x):
@@ -322,7 +322,7 @@
     t_out, s_out, e_res,
     flag_ref, point_ref, count_ref, tr, u, v, floor, low, mx, mn, ax, ay, az, rin, rout, adv,
     e_tr, e_u, e_v, e_floor, e_low, e_mx, e_mn, e_ax, e_ay, e_az, e_rin, e_rout, e_adv,
-    row_out, row_in, strip_out, fold_out, strip_in, corner_in,
+    row_out, row_in, strip_out, strip_in, side, fold_out, corner_in,
     load_sem, send_sem, recv_sem,
 ):
     n_lon, n_lat = lax.axis_size("lon"), lax.axis_size("lat")
@@ -331,46 +331,28 @@
     half = nk // 2
     east, west = lax.rem(lon + 1, n_lon), lax.rem(lon + n_lon - 1, n_lon)
     at_north, at_south = lat == n_lat - 1, lat == 0
-    fold_mid = n_lon - 1 - lon
-    fold_ne = lax.rem(2 * n_lon - 2 - lon, n_lon)
-    fold_nw = lax.rem(n_lon - lon, n_lon)
-
-    side = [(EAST, (east, lat)), (WEST, (west, lat))]
-    north = [(NORTH, (lon, lat + 1)), (NE, (east, lat + 1)), (NW, (west, lat + 1))]
-    south = [(SOUTH, (lon, lat - 1)), (SE, (east, lat - 1)), (SW, (west, lat - 1))]
-    folded = [(NORTH, (fold_mid, lat)), (NE, (fold_ne, lat)), (NW, (fold_nw, lat))]
-    ne_self, nw_self = fold_ne == lon, fold_nw == lon
-    not_self = {NORTH: True, NE: jnp.logical_not(ne_self), NW: jnp.logical_not(nw_self)}
+    to_east, to_west = (east, lat), (west, lat)
+    to_north, to_south, to_fold = (lon, lat + 1), (lon, lat - 1), (n_lon - 1 - lon, lat)
 
     barrier = pltpu.get_barrier_semaphore()
 
     def greet(where):
         pl.semaphore_signal(barrier, inc=1, device_id=where, device_id_type=MESH)
 
-    for _, where in side:
-        greet(where)
+    greet(to_east)
+    greet(to_west)
 
     @pl.when(jnp.logical_not(at_south))
     def _():
-        for _, where in south:
-            greet(where)
+        greet(to_south)
 
     @pl.when(jnp.logical_not(at_north))
     def _():
-        for _, where in north:
-            greet(where)
+        greet(to_north)
 
     @pl.when(at_north)
     def _():
-        greet(folded[0][1])
-
-        @pl.when(jnp.logical_not(ne_self))
-        def _():
-            greet(folded[1][1])
-
-        @pl.when(jnp.logical_not(nw_self))
-        def _():
-            greet(folded[2][1])
+        greet(to_fold)
 
     loads = [
         pltpu.make_async_copy(src, dst.at[:, 8:24, :], load_sem.at[i])
@@ -448,17 +430,7 @@
             )
         strip_out[half, row - 8 : row, :] = e_floor[rows, :]
 
-    @pl.when(at_north)
-    def _():
-        group_idx = lax.rem(lane8 + 7 - 2 * lax.rem(lane8 + 4, 8) + 128, 128)
-        sign = jnp.where(q_t, 1.0, -1.0)
-        for k in range(half + 1):
-            x = jnp.take_along_axis(strip_out[k, 8:16, :], group_idx, axis=1)
-            x = jnp.take_along_axis(x, 7 - sub8, axis=0)
-            fold_out[k] = x if k == half else x * sign
-
-    n_north = jnp.where(at_north, 3 - ne_self.astype(jnp.int32) - nw_self.astype(jnp.int32), 3)
-    pl.semaphore_wait(barrier, 2 + n_north + jnp.where(at_south, 0, 3))
+    pl.semaphore_wait(barrier, jnp.where(at_south, 3, 4))
 
     def send(src, dst, role, slot, where):
         return pltpu.make_async_remote_copy(
@@ -466,61 +438,29 @@
             device_id=where, device_id_type=MESH,
         )
 
-    corner = {NE: 0, NW: 1, SE: 2, SW: 3}
-
-    def to_rows(role, slot, where):
-        return send(row_out.at[0 if role == NORTH else 1], row_in.at[0 if slot == NORTH else 1], role, slot, where)
-
-    def to_corner(role, slot, where, fold=False):
-        src = fold_out if fold else strip_out.at[:, 8:16, :] if role in (NE, NW) else strip_out.at[:, 0:8, :]
-        return send(src, corner_in.at[corner[slot]], role, slot, where)
-
-    side_sends = [
-        send(strip_out, strip_in.at[0], WEST, EAST, (west, lat)),
-        send(strip_out, strip_in.at[1], EAST, WEST, (east, lat)),
-    ]
-    north_sends = [
-        to_rows(NORTH, SOUTH, north[0][1]),
-        to_corner(NE, SW, north[1][1]),
-        to_corner(NW, SE, north[2][1]),
-    ]
-    south_sends = [
-        to_rows(SOUTH, NORTH, south[0][1]),
-        to_corner(SE, NW, south[1][1]),
-        to_corner(SW, NE, south[2][1]),
-    ]
-    fold_sends = [
-        to_rows(NORTH, NORTH, folded[0][1]),
-        to_corner(NE, NE, folded[1][1], True),
-        to_corner(NW, NW, folded[2][1], True),
-    ]
-    ne_local = pltpu.make_async_copy(fold_out, corner_in.at[corner[NE]], send_sem.at[NE])
-    nw_local = pltpu.make_async_copy(fold_out, corner_in.at[corner[NW]], send_sem.at[NW])
+    rows_north = send(row_out.at[0], row_in.at[1], NORTH, SOUTH, to_north)
+    rows_fold = send(row_out.at[0], row_in.at[0], NORTH, NORTH, to_fold)
+    rows_south = send(row_out.at[1], row_in.at[0], SOUTH, NORTH, to_south)
+    strip_west = send(strip_out, strip_in.at[0], WEST, EAST, to_west)
+    strip_east = send(strip_out, strip_in.at[1], EAST, WEST, to_east)
+    corner_north = send(side.at[:, 8:16, :], corner_in.at[1], CORNER_NORTH, CORNER_SOUTH, to_north)
+    corner_fold = send(fold_out, corner_in.at[0], CORNER_NORTH, CORNER_NORTH, to_fold)
+    corner_south = send(side.at[:, 0:8, :], corner_in.at[0], CORNER_SOUTH, CORNER_NORTH, to_south)
+
+    strip_west.start()
+    strip_east.start()
 
     @pl.when(jnp.logical_not(at_south))
     def _():
-        for copy in south_sends:
-            copy.start()
+        rows_south.start()
 
     @pl.when(jnp.logical_not(at_north))
     def _():
-        for copy in north_sends:
-            copy.start()
+        rows_north.start()
 
     @pl.when(at_north)
     def _():
-        fold_sends[0].start()
-        for copy, local, own in ((fold_sends[1], ne_local, ne_self), (fold_sends[2], nw_local, nw_self)):
-            @pl.when(own)
-            def _():
-                local.start()
-
-            @pl.when(jnp.logical_not(own))
-            def _():
-                copy.start()
-
-    for copy in side_sends:
-        copy.start()
+        rows_fold.start()
 
     main = dict(
         split=False, t=[tr.at[0], tr.at[1]], u=u, v=v, f=floor,
@@ -540,21 +480,64 @@
 
     stage_diffuse(main, [(8, 16, 4, 12)], emit_inner)
 
+    strip_west.wait()
+    strip_east.wait()
+    from_east = lax.rem(lane8, 8) >= 4
+    for k in range(half + 1):
+        for at in (0, 8):
+            rows = slice(at, at + 8)
+            side[k, rows, :] = jnp.where(from_east, strip_in[0, k, rows, :], strip_in[1, k, rows, :])
+
+    @pl.when(jnp.logical_not(at_south))
+    def _():
+        corner_south.start()
+
+    @pl.when(jnp.logical_not(at_north))
+    def _():
+        corner_north.start()
+
+    @pl.when(at_north)
+    def _():
+        group_idx = lax.rem(lane8 + 7 - 2 * lax.rem(lane8 + 4, 8) + 128, 128)
+        sign = jnp.where(q_t, 1.0, -1.0)
+        for k in range(half + 1):
+            x = jnp.take_along_axis(side[k, 8:16, :], group_idx, axis=1)
+            x = jnp.take_along_axis(x, 7 - sub8, axis=0)
+            fold_out[k] = x if k == half else x * sign
+        corner_fold.start()
+
+    def strip_halo(row, ref, at):
+        rows = slice(row, row + 8)
+        for k in range(half + 1):
+            x = ref[k, at : at + 8, :]
+            if k == half:
+                e_floor[rows, :] = jnp.where(q_t, x, e_floor[rows, :])
+                continue
+            e_tr[k, rows, :] = jnp.where(q_t, x, e_tr[k, rows, :])
+            e_u[k, rows, :] = jnp.where(q_t, pltpu.roll(x, 120, 1), e_u[k, rows, :])
+            e_v[k, rows, :] = jnp.where(q_t, pltpu.roll(x, 112, 1), e_v[k, rows, :])
+
+    strip_halo(8, side, 0)
+    strip_halo(16, side, 8)
+
     @pl.when(at_south)
     def _():
         row_in[1] = jnp.zeros(row_in.shape[1:], jnp.float32)
+        corner_in[1] = jnp.zeros(corner_in.shape[1:], jnp.float32)
 
     @pl.when(jnp.logical_not(at_south))
     def _():
-        north_sends[0].wait_recv()
+        rows_south.wait_send()
+        rows_north.wait_recv()
 
     @pl.when(jnp.logical_not(at_north))
     def _():
-        south_sends[0].wait_recv()
+        rows_north.wait_send()
+        rows_south.wait_recv()
 
     @pl.when(at_north)
     def _():
-        fold_sends[0].wait_recv()
+        rows_fold.wait()
 
     for slot, row in ((1, 4), (0, 24)):
         for g, (a, b) in enumerate(fields):
@@ -575,58 +558,25 @@
 
     stage_diffuse(main, [(4, 8, 4, 8), (16, 8, 4, 8)], emit_outer)
 
-    @pl.when(at_south)
-    def _():
-        corner_in[corner[SE]] = jnp.zeros(corner_in.shape[1:], jnp.float32)
-        corner_in[corner[SW]] = jnp.zeros(corner_in.shape[1:], jnp.float32)
-
-    @pl.when(jnp.logical_not(at_south))
-    def _():
-        for copy in north_sends[1:]:
-            copy.wait_recv()
-        for copy in south_sends:
-            copy.wait_send()
-
-    @pl.when(jnp.logical_not(at_north))
-    def _():
-        for copy in south_sends[1:]:
-            copy.wait_recv()
-        for copy in north_sends:
-            copy.wait_send()
-
-    @pl.when(at_north)
-    def _():
-        fold_sends[0].wait_send()
-        for copy, local, own in ((fold_sends[1], ne_local, ne_self), (fold_sends[2], nw_local, nw_self)):
-            @pl.when(own)
-            def _():
-                local.wait()
-
-            @pl.when(jnp.logical_not(own))
-            def _():
-                copy.wait()
-
-    for copy in side_sends:
-        copy.wait()
-
     strip_tile(0)
     strip_tile(24)
-    from_east = lax.rem(lane8, 8) >= 4
-    for row, east_ref, west_ref, at in (
-        (0, corner_in.at[corner[SE]], corner_in.at[corner[SW]], 0),
-        (8, strip_in.at[0], strip_in.at[1], 0),
-        (16, strip_in.at[0], strip_in.at[1], 8),
-        (24, corner_in.at[corner[NE]], corner_in.at[corner[NW]], 0),
-    ):
-        rows = slice(row, row + 8)
-        for k in range(half + 1):
-            x = jnp.where(from_east, east_ref[k, at : at + 8, :], west_ref[k, at : at + 8, :])
-            if k == half:
-                e_floor[rows, :] = jnp.where(q_t, x, e_floor[rows, :])
-                continue
-            e_tr[k, rows, :] = jnp.where(q_t, x, e_tr[k, rows, :])
-            e_u[k, rows, :] = jnp.where(q_t, pltpu.roll(x, 120, 1), e_u[k, rows, :])
-            e_v[k, rows, :] = jnp.where(q_t, pltpu.roll(x, 112, 1), e_v[k, rows, :])
+
+    @pl.when(jnp.logical_not(at_south))
+    def _():
+        corner_south.wait_send()
+        corner_north.wait_recv()
+
+    @pl.when(jnp.logical_not(at_north))
+    def _():
+        corner_north.wait_send()
+        corner_south.wait_recv()
+
+    @pl.when(at_north)
+    def _():
+        corner_fold.wait()
+
+    strip_halo(0, corner_in.at[1], 0)
+    strip_halo(24, corner_in.at[0], 0)
 
     def strip_density(one):
         x = one[0]
@@ -685,9 +635,9 @@
             *[vm(nk // 2, 32, 128) for _ in range(3)], vm(32, 128),
             *[vm(nk // 2, 32, 128) for _ in range(9)],
             vm(2, 2 * nk + 1, 8, 128), vm(2, 2 * nk + 1, 8, 128),
-            vm(nk // 2 + 1, 16, 128), vm(nk // 2 + 1, 8, 128),
-            vm(2, nk // 2 + 1, 16, 128), vm(4, nk // 2 + 1, 8, 128),
-            pltpu.SemaphoreType.DMA((7,)), pltpu.SemaphoreType.DMA((8,)), pltpu.SemaphoreType.DMA((8,)),
+            vm(nk // 2 + 1, 16, 128), vm(2, nk // 2 + 1, 16, 128), vm(nk // 2 + 1, 16, 128),
+            vm(nk // 2 + 1, 8, 128), vm(2, nk // 2 + 1, 8, 128),
+            pltpu.SemaphoreType.DMA((7,)), pltpu.SemaphoreType.DMA((6,)), pltpu.SemaphoreType.DMA((6,)),
         ],
         compiler_params=pltpu.CompilerParams(
             collective_id=0, has_side_effects=True, vmem_limit_bytes=60 * 1024 * 1024

time: 19.9 us -> 18 us (0.905)
  the two profiles are of different devices: /device:TPU:64 before, /device:TPU:96 now
where the time goes in v4:
time: 18 us; the launch traced here: 17.8 us
  Pallas kernels  16.5 us (92%)
  between operations  1.29 us (7%)
    pallas_call x1, Pallas kernels, on_device(): pl.pallas_call(kernel, out_shape=(part, part, pltpu.VMEM((nk // 2, *t.sha...  15.7 us
    pallas_call x1, Pallas kernels, on_device(): pl.pallas_call(finish, out_shape=(result, result), in_specs=[whole] * 3,...  0.79 us

profile of v4, /device:TPU:96, one launch (start us, length us, event | category | flops | bytes accessed | tf_op | source)
XLA Modules:
  0.0 17.8 jit_solution(10272968617519215583)
XLA Ops:
  1.3 15.7 %shard_map.86 = (f32[12,16,128]{2,1,0:T(8,128)S(1)}, f32[12,16,128]{2,1,0:T(8,128)S(1)}, f32[6,16,128]{2,1,0:T(8,128)S(1)}) custom-call(f32[12,16,128]{2,1,0:T(8,128)} %t_hbm.1, f32[12,16,128]{2,1,0:T(8,128)} %s_hbm.1, f32[12,16,128]{2,1,0:T(8,128)} %u_hbm.1, f32[12,16,128]{2,1,0:T(8,128)} %v_hbm.1, s32[1,1]{1,0:T(1,128)S(6)} %copy.9.flag_hbm, ...), custom_call_target="tpu_custom_call" | custom-call | tf_op jit(solution)/shard_map/pallas_call | solution.py:626
  17.0 0.8 %shard_map.87 = (f32[12,16,128]{2,1,0:T(8,128)}, f32[12,16,128]{2,1,0:T(8,128)}) custom-call(f32[12,16,128]{2,1,0:T(8,128)S(1)} %get-tuple-element.5.t_ref, f32[12,16,128]{2,1,0:T(8,128)S(1)} %get-tuple-element.6.s_ref, f32[6,16,128]{2,1,0:T(8,128)S(1)} %get-tuple-element.7.e_res), custom_call_target="tpu_custom_call" | custom-call | tf_op jit(solution)/shard_map/pallas_call | solution.py:647

commit v5 on v4

--- a/solution.py
+++ b/solution.py
@@ -20,7 +20,8 @@
 FACE_SCALE = 0.25 * time_step
 DIFF_SCALE = 0.25 * time_step * diffusivity
 
-EAST, WEST, NORTH, SOUTH, CORNER_NORTH, CORNER_SOUTH = range(6)
+EAST, WEST, NORTH, SOUTH, NE, NW, SE, SW = range(8)
+CORNER = {NE: 0, NW: 1, SE: 2, SW: 3}
 
 
 def east_of(x):
@@ -69,7 +70,7 @@
     return jnp.where(upper_lanes(n), pltpu.roll(ref[0, r0 : r0 + n, :], 96, 1), ref[last, r0 : r0 + n, :])
 
 
-def upward(z, body, carry, unroll):
+def upward(z, body, carry):
     nk = z["u"].shape[0]
     if z["split"]:
         for k in range(nk - 1, -1, -1):
@@ -80,7 +81,7 @@
         k = nk - 1 - i
         return body(k, k.astype(jnp.float32), carry)
 
-    return lax.fori_loop(0, nk, step, carry, unroll=unroll)
+    return lax.fori_loop(0, nk, step, carry, unroll=nk // 2)
 
 
 def nothing(z, wins):
@@ -145,7 +146,7 @@
                 up, c = t[nk - 1, r0 : r0 + n, :], below(z, t, nk - 1, r0, n)
                 flows.append(w * (c + up) - jnp.abs(w) * (up - c))
         start.append((w, tuple(flows)))
-    upward(z, body, tuple(start), nk)
+    upward(z, body, tuple(start))
 
 
 def stage_ratio(z, wins):
@@ -183,7 +184,7 @@
     start = nothing(z, wins)
     if z["split"]:
         start = tuple(tuple(to_upper(a[0, r0 : r0 + n, :]) for a in z["az"]) for r0, n, _, _ in wins)
-    upward(z, body, start, nk)
+    upward(z, body, start)
 
 
 def limited(anti, r_in, r_out, far_in, far_out):
@@ -222,7 +223,7 @@
     start = nothing(z, wins)
     if z["split"]:
         start = tuple(tuple(to_upper(rise(m, 0, r0, n)) for m in range(len(z["t"]))) for r0, n, _, _ in wins)
-    upward(z, body, start, nk)
+    upward(z, body, start)
 
 
 def clip_slope(x):
@@ -306,7 +307,7 @@
         if z["split"]:
             first = jax.tree.map(to_upper, vertical(0, jnp.float32(0), r0, n, f, far_n))
         start.append((first, xs, xs))
-    last = upward(z, body, tuple(start), nk // 2)
+    last = upward(z, body, tuple(start))
     for wi, ((r0, n, _, _), (f, *_), (_, parts, tops)) in enumerate(zip(wins, stat, last)):
         for m in range(nt):
             top = tops[m]
@@ -322,8 +323,8 @@
     t_out, s_out, e_res,
     flag_ref, point_ref, count_ref, tr, u, v, floor, low, mx, mn, ax, ay, az, rin, rout, adv,
     e_tr, e_u, e_v, e_floor, e_low, e_mx, e_mn, e_ax, e_ay, e_az, e_rin, e_rout, e_adv,
-    row_out, row_in, strip_out, strip_in, side, fold_out, corner_in,
-    load_sem, send_sem, recv_sem,
+    row_out, row_in, strip_out, strip_in, fold_out, corner_in,
+    load_sem, send_sem, recv_sem, ready,
 ):
     n_lon, n_lat = lax.axis_size("lon"), lax.axis_size("lat")
     lon, lat = lax.axis_index("lon"), lax.axis_index("lat")
@@ -333,6 +334,8 @@
     at_north, at_south = lat == n_lat - 1, lat == 0
     to_east, to_west = (east, lat), (west, lat)
     to_north, to_south, to_fold = (lon, lat + 1), (lon, lat - 1), (n_lon - 1 - lon, lat)
+    fold_ne, fold_nw = lax.rem(2 * n_lon - 2 - lon, n_lon), lax.rem(n_lon - lon, n_lon)
+    ne_self, nw_self = fold_ne == lon, fold_nw == lon
 
     barrier = pltpu.get_barrier_semaphore()
 
@@ -368,35 +371,7 @@
         copy.wait()
     floor[8:24, :] = (count_ref[...] * point_ref[...] * flag_ref[...]).astype(jnp.float32)
 
-    fields = ((tr.at[0], tr.at[1]), (u, v))
-    for g, (a, b) in enumerate(fields):
-        for k in range(nk):
-            row_out[1, g * nk + k, 0:4, :] = a[k, 8:12, :]
-            row_out[1, g * nk + k, 4:8, :] = b[k, 8:12, :]
-    row_out[1, 2 * nk, 0:4, :] = floor[8:12, :]
-
-    @pl.when(jnp.logical_not(at_north))
-    def _():
-        for g, (a, b) in enumerate(fields):
-            for k in range(nk):
-                row_out[0, g * nk + k, 0:4, :] = a[k, 20:24, :]
-                row_out[0, g * nk + k, 4:8, :] = b[k, 20:24, :]
-        row_out[0, 2 * nk, 0:4, :] = floor[20:24, :]
-
     lane8, sub8 = lane_iota(8), lax.broadcasted_iota(jnp.int32, (8, 128), 0)
-
-    @pl.when(at_north)
-    def _():
-        def turned(x):
-            x = jnp.take_along_axis(x, 127 - lane8, axis=1)
-            return jnp.take_along_axis(x, 7 - sub8, axis=0)
-
-        for g, (a, b) in enumerate(fields):
-            sign = 1.0 if g == 0 else -1.0
-            for k in range(nk):
-                row_out[0, g * nk + k, 0:4, :] = sign * turned(a[k, 16:24, :])[0:4]
-                row_out[0, g * nk + k, 4:8, :] = sign * turned(b[k, 16:24, :])[0:4]
-        row_out[0, 2 * nk, 0:4, :] = turned(floor[16:24, :])[0:4]
 
     p = lax.rem(lane8, 32)
     shift = jnp.where(p < 12, 116, jnp.where(p < 16, -12, jnp.where(p < 20, 108, -20)))
@@ -432,6 +407,9 @@
 
     pl.semaphore_wait(barrier, jnp.where(at_south, 3, 4))
 
+    pl.semaphore_signal(ready.at[1], inc=1, device_id=to_east, device_id_type=MESH)
+    pl.semaphore_signal(ready.at[0], inc=1, device_id=to_west, device_id_type=MESH)
+
     def send(src, dst, role, slot, where):
         return pltpu.make_async_remote_copy(
             src_ref=src, dst_ref=dst, send_sem=send_sem.at[role], recv_sem=recv_sem.at[slot],
@@ -443,13 +421,36 @@
     rows_south = send(row_out.at[1], row_in.at[0], SOUTH, NORTH, to_south)
     strip_west = send(strip_out, strip_in.at[0], WEST, EAST, to_west)
     strip_east = send(strip_out, strip_in.at[1], EAST, WEST, to_east)
-    corner_north = send(side.at[:, 8:16, :], corner_in.at[1], CORNER_NORTH, CORNER_SOUTH, to_north)
-    corner_fold = send(fold_out, corner_in.at[0], CORNER_NORTH, CORNER_NORTH, to_fold)
-    corner_south = send(side.at[:, 0:8, :], corner_in.at[0], CORNER_SOUTH, CORNER_NORTH, to_south)
+
+    def corner(src, role, slot, where):
+        return send(src, corner_in.at[CORNER[slot]], role, slot, where)
+
+    upper_rows, lower_rows = strip_out.at[:, 8:16, :], strip_out.at[:, 0:8, :]
+    corners_north = (corner(upper_rows, NE, SW, (east, lat + 1)), corner(upper_rows, NW, SE, (west, lat + 1)))
+    corners_south = (corner(lower_rows, SE, NW, (east, lat - 1)), corner(lower_rows, SW, NE, (west, lat - 1)))
+    corners_fold = (
+        (corner(fold_out, NE, NE, (fold_ne, lat)), pltpu.make_async_copy(fold_out, corner_in.at[CORNER[NE]], send_sem.at[NE]), ne_self),
+        (corner(fold_out, NW, NW, (fold_nw, lat)), pltpu.make_async_copy(fold_out, corner_in.at[CORNER[NW]], send_sem.at[NW]), nw_self),
+    )
 
     strip_west.start()
     strip_east.start()
 
+    fields = ((tr.at[0], tr.at[1]), (u, v))
+    for side_no, row in ((0, 20), (1, 8)):
+        for g, (a, b) in enumerate(fields):
+            for k in range(nk):
+                row_out[side_no, g * nk + k, 0:4, :] = a[k, row : row + 4, :]
+                row_out[side_no, g * nk + k, 4:8, :] = b[k, row : row + 4, :]
+        row_out[side_no, 2 * nk, 0:4, :] = floor[row : row + 4, :]
+
+    @pl.when(at_north)
+    def _():
+        for k in range(2 * nk + 1):
+            x = jnp.take_along_axis(row_out[0, k], 127 - lane8, axis=1)
+            x = jnp.take_along_axis(x, 3 - lax.rem(sub8, 4) + jnp.where(sub8 < 4, 0, 4), axis=0)
+            row_out[0, k] = -x if nk <= k < 2 * nk else x
+
     @pl.when(jnp.logical_not(at_south))
     def _():
         rows_south.start()
@@ -461,6 +462,31 @@
     @pl.when(at_north)
     def _():
         rows_fold.start()
+
+    pl.semaphore_wait(ready.at[0], 1)
+    pl.semaphore_wait(ready.at[1], 1)
+
+    @pl.when(jnp.logical_not(at_south))
+    def _():
+        for copy in corners_south:
+            copy.start()
+
+    @pl.when(jnp.logical_not(at_north))
+    def _():
+        for copy in corners_north:
+            copy.start()
+
+    @pl.when(at_north)
+    def _():
+        group_idx = lax.rem(lane8 + 7 - 2 * lax.rem(lane8 + 4, 8) + 128, 128)
+        sign = jnp.where(q_t, 1.0, -1.0)
+        for k in range(half + 1):
+            x = jnp.take_along_axis(strip_out[k, 8:16, :], group_idx, axis=1)
+            x = jnp.take_along_axis(x, 7 - sub8, axis=0)
+            fold_out[k] = x if k == half else x * sign
+        for copy, local, own in corners_fold:
+            pl.when(own)(local.start)
+            pl.when(jnp.logical_not(own))(copy.start)
 
     main = dict(
         split=False, t=[tr.at[0], tr.at[1]], u=u, v=v, f=floor,
@@ -483,33 +509,11 @@
     strip_west.wait()
     strip_east.wait()
     from_east = lax.rem(lane8, 8) >= 4
-    for k in range(half + 1):
-        for at in (0, 8):
-            rows = slice(at, at + 8)
-            side[k, rows, :] = jnp.where(from_east, strip_in[0, k, rows, :], strip_in[1, k, rows, :])
-
-    @pl.when(jnp.logical_not(at_south))
-    def _():
-        corner_south.start()
-
-    @pl.when(jnp.logical_not(at_north))
-    def _():
-        corner_north.start()
-
-    @pl.when(at_north)
-    def _():
-        group_idx = lax.rem(lane8 + 7 - 2 * lax.rem(lane8 + 4, 8) + 128, 128)
-        sign = jnp.where(q_t, 1.0, -1.0)
-        for k in range(half + 1):
-            x = jnp.take_along_axis(side[k, 8:16, :], group_idx, axis=1)
-            x = jnp.take_along_axis(x, 7 - sub8, axis=0)
-            fold_out[k] = x if k == half else x * sign
-        corner_fold.start()
-
-    def strip_halo(row, ref, at):
+
+    def strip_halo(row, east_ref, west_ref, at):
         rows = slice(row, row + 8)
         for k in range(half + 1):
-            x = ref[k, at : at + 8, :]
+            x = jnp.where(from_east, east_ref[k, at : at + 8, :], west_ref[k, at : at + 8, :])
             if k == half:
                 e_floor[rows, :] = jnp.where(q_t, x, e_floor[rows, :])
                 continue
@@ -517,13 +521,14 @@
             e_u[k, rows, :] = jnp.where(q_t, pltpu.roll(x, 120, 1), e_u[k, rows, :])
             e_v[k, rows, :] = jnp.where(q_t, pltpu.roll(x, 112, 1), e_v[k, rows, :])
 
-    strip_halo(8, side, 0)
-    strip_halo(16, side, 8)
+    strip_halo(8, strip_in.at[0], strip_in.at[1], 0)
+    strip_halo(16, strip_in.at[0], strip_in.at[1], 8)
 
     @pl.when(at_south)
     def _():
         row_in[1] = jnp.zeros(row_in.shape[1:], jnp.float32)
-        corner_in[1] = jnp.zeros(corner_in.shape[1:], jnp.float32)
+        for slot in (SE, SW):
+            corner_in[CORNER[slot]] = jnp.zeros(corner_in.shape[1:], jnp.float32)
 
     @pl.when(jnp.logical_not(at_south))
     def _():
@@ -563,20 +568,26 @@
 
     @pl.when(jnp.logical_not(at_south))
     def _():
-        corner_south.wait_send()
-        corner_north.wait_recv()
+        for copy in corners_south:
+            copy.wait_send()
+        for copy in corners_north:
+            copy.wait_recv()
 
     @pl.when(jnp.logical_not(at_north))
     def _():
-        corner_north.wait_send()
-        corner_south.wait_recv()
+        for copy in corners_north:
+            copy.wait_send()
+        for copy in corners_south:
+            copy.wait_recv()
 
     @pl.when(at_north)
     def _():
-        corner_fold.wait()
-
-    strip_halo(0, corner_in.at[1], 0)
-    strip_halo(24, corner_in.at[0], 0)
+        for copy, local, own in corners_fold:
+            pl.when(own)(local.wait)
+            pl.when(jnp.logical_not(own))(copy.wait)
+
+    strip_halo(0, corner_in.at[CORNER[SE]], corner_in.at[CORNER[SW]], 0)
+    strip_halo(24, corner_in.at[CORNER[NE]], corner_in.at[CORNER[NW]], 0)
 
     def strip_density(one):
         x = one[0]
@@ -635,9 +646,10 @@
             *[vm(nk // 2, 32, 128) for _ in range(3)], vm(32, 128),
             *[vm(nk // 2, 32, 128) for _ in range(9)],
             vm(2, 2 * nk + 1, 8, 128), vm(2, 2 * nk + 1, 8, 128),
-            vm(nk // 2 + 1, 16, 128), vm(2, nk // 2 + 1, 16, 128), vm(nk // 2 + 1, 16, 128),
-            vm(nk // 2 + 1, 8, 128), vm(2, nk // 2 + 1, 8, 128),
-            pltpu.SemaphoreType.DMA((7,)), pltpu.SemaphoreType.DMA((6,)), pltpu.SemaphoreType.DMA((6,)),
+            vm(nk // 2 + 1, 16, 128), vm(2, nk // 2 + 1, 16, 128),
+            vm(nk // 2 + 1, 8, 128), vm(4, nk // 2 + 1, 8, 128),
+            pltpu.SemaphoreType.DMA((7,)), pltpu.SemaphoreType.DMA((8,)), pltpu.SemaphoreType.DMA((8,)),
+            pltpu.SemaphoreType.REGULAR((2,)),
         ],
         compiler_params=pltpu.CompilerParams(
             collective_id=0, has_side_effects=True, vmem_limit_bytes=60 * 1024 * 1024

time: 18 us -> 17.7 us (0.983)
  Pallas kernels: 16.5 us -> 16.3 us
    pallas_call x1, Pallas kernels: 15.7 us -> 15.5 us  [on_device(): pl.pallas_call(kernel, out_shape=(part, part, pltpu.VMEM((nk // 2, *t.sha...]
where the time goes in v5:
time: 17.7 us; the launch traced here: 17.6 us
  Pallas kernels  16.3 us (92%)
  between operations  1.29 us (7%)
    pallas_call x1, Pallas kernels, on_device(): pl.pallas_call(kernel, out_shape=(part, part, pltpu.VMEM((nk // 2, *t.sha...  15.5 us
    pallas_call x1, Pallas kernels, on_device(): pl.pallas_call(finish, out_shape=(result, result), in_specs=[whole] * 3,...  0.79 us

profile of v5, /device:TPU:96, one launch (start us, length us, event | category | flops | bytes accessed | tf_op | source)
XLA Modules:
  0.0 17.6 jit_solution(8787185573070771621)
XLA Ops:
  1.3 15.5 %shard_map.86 = (f32[12,16,128]{2,1,0:T(8,128)S(1)}, f32[12,16,128]{2,1,0:T(8,128)S(1)}, f32[6,16,128]{2,1,0:T(8,128)S(1)}) custom-call(f32[12,16,128]{2,1,0:T(8,128)} %t_hbm.1, f32[12,16,128]{2,1,0:T(8,128)} %s_hbm.1, f32[12,16,128]{2,1,0:T(8,128)} %u_hbm.1, f32[12,16,128]{2,1,0:T(8,128)} %v_hbm.1, s32[1,1]{1,0:T(1,128)S(6)} %copy.9.flag_hbm, ...), custom_call_target="tpu_custom_call" | custom-call | tf_op jit(solution)/shard_map/pallas_call | solution.py:637
  16.8 0.8 %shard_map.87 = (f32[12,16,128]{2,1,0:T(8,128)}, f32[12,16,128]{2,1,0:T(8,128)}) custom-call(f32[12,16,128]{2,1,0:T(8,128)S(1)} %get-tuple-element.5.t_ref, f32[12,16,128]{2,1,0:T(8,128)S(1)} %get-tuple-element.6.s_ref, f32[6,16,128]{2,1,0:T(8,128)S(1)} %get-tuple-element.7.e_res), custom_call_target="tpu_custom_call" | custom-call | tf_op jit(solution)/shard_map/pallas_call | solution.py:659

commit v6 on v5

--- a/solution.py
+++ b/solution.py
@@ -407,8 +407,12 @@
 
     pl.semaphore_wait(barrier, jnp.where(at_south, 3, 4))
 
-    pl.semaphore_signal(ready.at[1], inc=1, device_id=to_east, device_id_type=MESH)
-    pl.semaphore_signal(ready.at[0], inc=1, device_id=to_west, device_id_type=MESH)
+    def tell(slot, where):
+        pl.semaphore_signal(ready.at[slot], inc=1, device_id=where, device_id_type=MESH)
+
+    pl.when(jnp.logical_not(at_south))(lambda: tell(0, to_south))
+    pl.when(jnp.logical_not(at_north))(lambda: tell(1, to_north))
+    pl.when(at_north)(lambda: tell(0, to_fold))
 
     def send(src, dst, role, slot, where):
         return pltpu.make_async_remote_copy(
@@ -463,13 +467,13 @@
     def _():
         rows_fold.start()
 
-    pl.semaphore_wait(ready.at[0], 1)
-    pl.semaphore_wait(ready.at[1], 1)
-
     @pl.when(jnp.logical_not(at_south))
     def _():
+        pl.semaphore_wait(ready.at[1], 1)
         for copy in corners_south:
             copy.start()
+
+    pl.semaphore_wait(ready.at[0], 1)
 
     @pl.when(jnp.logical_not(at_north))
     def _():

time: 17.7 us -> 16.8 us (0.949)
  the two profiles are of different devices: /device:TPU:96 before, /device:TPU:225 now
where the time goes in v6:
time: 16.8 us; the launch traced here: 16.7 us
  Pallas kernels  15.4 us (92%)
  between operations  1.29 us (8%)
    pallas_call x1, Pallas kernels, on_device(): pl.pallas_call(kernel, out_shape=(part, part, pltpu.VMEM((nk // 2, *t.sha...  14.6 us
    pallas_call x1, Pallas kernels, on_device(): pl.pallas_call(finish, out_shape=(result, result), in_specs=[whole] * 3,...  0.79 us

profile of v6, /device:TPU:225, one launch (start us, length us, event | category | flops | bytes accessed | tf_op | source)
XLA Modules:
  0.0 16.7 jit_solution(8756302599010963092)
XLA Ops:
  1.3 14.6 %shard_map.86 = (f32[12,16,128]{2,1,0:T(8,128)S(1)}, f32[12,16,128]{2,1,0:T(8,128)S(1)}, f32[6,16,128]{2,1,0:T(8,128)S(1)}) custom-call(f32[12,16,128]{2,1,0:T(8,128)} %t_hbm.1, f32[12,16,128]{2,1,0:T(8,128)} %s_hbm.1, f32[12,16,128]{2,1,0:T(8,128)} %u_hbm.1, f32[12,16,128]{2,1,0:T(8,128)} %v_hbm.1, s32[1,1]{1,0:T(1,128)S(6)} %copy.9.flag_hbm, ...), custom_call_target="tpu_custom_call" | custom-call | tf_op jit(solution)/shard_map/pallas_call | solution.py:641
  15.9 0.8 %shard_map.87 = (f32[12,16,128]{2,1,0:T(8,128)}, f32[12,16,128]{2,1,0:T(8,128)}) custom-call(f32[12,16,128]{2,1,0:T(8,128)S(1)} %get-tuple-element.5.t_ref, f32[12,16,128]{2,1,0:T(8,128)S(1)} %get-tuple-element.6.s_ref, f32[6,16,128]{2,1,0:T(8,128)S(1)} %get-tuple-element.7.e_res), custom_call_target="tpu_custom_call" | custom-call | tf_op jit(solution)/shard_map/pallas_call | solution.py:663

commit v7 on v6

--- a/solution.py
+++ b/solution.py
@@ -333,7 +333,8 @@
     east, west = lax.rem(lon + 1, n_lon), lax.rem(lon + n_lon - 1, n_lon)
     at_north, at_south = lat == n_lat - 1, lat == 0
     to_east, to_west = (east, lat), (west, lat)
-    to_north, to_south, to_fold = (lon, lat + 1), (lon, lat - 1), (n_lon - 1 - lon, lat)
+    above_lat, below_lat = lax.rem(lat + 1, n_lat), lax.rem(lat + n_lat - 1, n_lat)
+    to_north, to_south, to_fold = (lon, above_lat), (lon, below_lat), (n_lon - 1 - lon, lat)
     fold_ne, fold_nw = lax.rem(2 * n_lon - 2 - lon, n_lon), lax.rem(n_lon - lon, n_lon)
     ne_self, nw_self = fold_ne == lon, fold_nw == lon
 
@@ -430,8 +431,8 @@
         return send(src, corner_in.at[CORNER[slot]], role, slot, where)
 
     upper_rows, lower_rows = strip_out.at[:, 8:16, :], strip_out.at[:, 0:8, :]
-    corners_north = (corner(upper_rows, NE, SW, (east, lat + 1)), corner(upper_rows, NW, SE, (west, lat + 1)))
-    corners_south = (corner(lower_rows, SE, NW, (east, lat - 1)), corner(lower_rows, SW, NE, (west, lat - 1)))
+    corners_north = (corner(upper_rows, NE, SW, (east, above_lat)), corner(upper_rows, NW, SE, (west, above_lat)))
+    corners_south = (corner(lower_rows, SE, NW, (east, below_lat)), corner(lower_rows, SW, NE, (west, below_lat)))
     corners_fold = (
         (corner(fold_out, NE, NE, (fold_ne, lat)), pltpu.make_async_copy(fold_out, corner_in.at[CORNER[NE]], send_sem.at[NE]), ne_self),
         (corner(fold_out, NW, NW, (fold_nw, lat)), pltpu.make_async_copy(fold_out, corner_in.at[CORNER[NW]], send_sem.at[NW]), nw_self),

time: 16.8 us -> 16.8 us (level)
  no operation moved by 1% of the time
where the time goes in v7:
time: 16.8 us; the launch traced here: 16.7 us
  Pallas kernels  15.4 us (92%)
  between operations  1.29 us (8%)
    pallas_call x1, Pallas kernels, on_device(): pl.pallas_call(kernel, out_shape=(part, part, pltpu.VMEM((nk // 2, *t.sha...  14.6 us
    pallas_call x1, Pallas kernels, on_device(): pl.pallas_call(finish, out_shape=(result, result), in_specs=[whole] * 3,...  0.79 us

profile of v7, /device:TPU:225, one launch (start us, length us, event | category | flops | bytes accessed | tf_op | source)
XLA Modules:
  0.0 16.7 jit_solution(16565287681088368235)
XLA Ops:
  1.3 14.6 %shard_map.86 = (f32[12,16,128]{2,1,0:T(8,128)S(1)}, f32[12,16,128]{2,1,0:T(8,128)S(1)}, f32[6,16,128]{2,1,0:T(8,128)S(1)}) custom-call(f32[12,16,128]{2,1,0:T(8,128)} %t_hbm.1, f32[12,16,128]{2,1,0:T(8,128)} %s_hbm.1, f32[12,16,128]{2,1,0:T(8,128)} %u_hbm.1, f32[12,16,128]{2,1,0:T(8,128)} %v_hbm.1, s32[1,1]{1,0:T(1,128)S(6)} %copy.9.flag_hbm, ...), custom_call_target="tpu_custom_call" | custom-call | tf_op jit(solution)/shard_map/pallas_call | solution.py:642
  15.9 0.8 %shard_map.87 = (f32[12,16,128]{2,1,0:T(8,128)}, f32[12,16,128]{2,1,0:T(8,128)}) custom-call(f32[12,16,128]{2,1,0:T(8,128)S(1)} %get-tuple-element.5.t_ref, f32[12,16,128]{2,1,0:T(8,128)S(1)} %get-tuple-element.6.s_ref, f32[6,16,128]{2,1,0:T(8,128)S(1)} %get-tuple-element.7.e_res), custom_call_target="tpu_custom_call" | custom-call | tf_op jit(solution)/shard_map/pallas_call | solution.py:664
